TPU v7x, 32 devices: a whole 2x2x4 slice. The times are simulated.
32 devices in a mesh: group: 2 (over y), shot: 4 (over z), line: 2 (over x), tm: 2 (over core).
Axes of the slice: x: 2, y: 2, z: 4, core: 2. Of those that a mesh axis runs over, the one named last changes fastest.
Arguments:
- initial_guess: bfloat16 [8, 256, 1024], P(('group', 'shot'), 'line', 'tm'), parts along dimension 0
- measured_mixtures: bfloat16 [4, 256, 1024], P('group', 'line'), parts along dimension 0
- launch_lags: int32 [8], P('group'), parts along dimension 0, may hold values from 0 to 127, as said below
- source_launch_order: int32 [8], P('group'), parts along dimension 0, may hold values from 0 to 3, each once
- station_portion_tallies: int32 [16], P('group'), parts along dimension 0, may hold values from 1 to 32, 128 in all
- source_entry_kernel: bfloat16 [4, 3, 64], replicated, may hold values from -1.75 to 1.75
- source_spaced_kernel: bfloat16 [3, 64, 64], replicated, may hold values from -0.4375 to 0.4375
- source_exit_kernel: bfloat16 [4, 64], replicated, may hold values from -0.5 to 0.5
- source_inner_offsets: float32 [2, 64], replicated, may hold values from -3 to 3
- station_entry_kernel: bfloat16 [4, 3, 64], replicated, may hold values from -1.75 to 1.75
- station_spaced_kernel: bfloat16 [3, 64, 64], replicated, may hold values from -0.4375 to 0.4375
- station_exit_kernel: bfloat16 [4, 64], replicated, may hold values from -0.5 to 0.5
- station_inner_offsets: float32 [2, 64], replicated, may hold values from -3 to 3
- learned_pace_factors: float32 [2], replicated, may hold values from 0.3 to 0.8
Outputs:
- deblended: bfloat16 [8, 256, 1024], P(('group', 'shot'), 'line', 'tm'), parts along dimension 0
There are 2 independent parts, one for each index of `group`. A program takes and returns all parts, laid end to end along the dimension named above; an argument that names none is the same for every part. Nothing has to cross between parts.
Inputs may be any that keep to these rules, and one draw needn't show every extreme that they name: `launch_lags`: 0 and 127 both occur. `source_launch_order`: each shot once. `station_portion_tallies`: the counts sum to 128 and the largest equals 32.
All inputs are finite; a program needn't handle non-finite values.
Results may differ from a plain program's by a relative error of at most 0.013.
Values may be sent and summed in bfloat16 or wider, within the bound.
A program may use at most 64 MiB of HBM per device.

v0:
```python
import functools
import math

import jax
import jax.numpy as jnp
from jax import lax
from jax.experimental import pallas as pl
from jax.experimental.pallas import tpu as pltpu
from jax.sharding import PartitionSpec as P

RPL = 16
ITERS = 2
EPSILON = 1e-05
C = 8
PACK = 4
TAPS = (1, 2, 3, 0)
F32, BF16 = jnp.float32, jnp.bfloat16
AXES = ("shot", "line", "tm")


def ahead(x, k):
    edge = pltpu.roll(x[:k], C - 1, 1)
    edge = jnp.where(lax.broadcasted_iota(jnp.int32, edge.shape, 1) == C - 1, 0.0, edge)
    return edge if k == x.shape[0] else jnp.concatenate([x[k:], edge], axis=0)


def behind(x, k):
    edge = pltpu.roll(x[x.shape[0] - k :], 1, 1)
    edge = jnp.where(lax.broadcasted_iota(jnp.int32, edge.shape, 1) == 0, 0.0, edge)
    return edge if k == x.shape[0] else jnp.concatenate([edge, x[: x.shape[0] - k]], axis=0)


def even_lanes(shape):
    return lax.broadcasted_iota(jnp.int32, shape, len(shape) - 1) < shape[-1] // 2


def net(x, w_in, w_mid, w_out, bias, total):
    planes, _, lanes = x.shape
    rows = planes * C
    side = jnp.where(even_lanes(x.shape), ahead(x, 1), behind(x, 1))
    z = jnp.concatenate([x, side], axis=2).astype(BF16).reshape(rows, 2 * lanes)
    total[...] = jnp.zeros_like(total)
    wide = w_in.shape[2]

    def step(q, carry):
        h = jnp.dot(z, w_in[q], preferred_element_type=F32)
        h = jnp.maximum(h + bias[0:1, :], 0.0)
        cube = h.reshape(planes, C, wide)
        first = ahead(cube[:2], 2).reshape(2 * C, wide).astype(BF16)
        last = behind(cube[planes - 2 :], 2).reshape(2 * C, wide).astype(BF16)
        hb = h.astype(BF16)
        early = jnp.concatenate([last, hb[: rows - 2 * C]], axis=0)
        late = jnp.concatenate([hb[2 * C :], first], axis=0)
        g = jnp.dot(jnp.concatenate([early, hb, late], axis=1), w_mid[...], preferred_element_type=F32)
        g = jnp.maximum(g + bias[1:2, :], 0.0).astype(BF16)
        total[...] += jnp.dot(g, w_out[q], preferred_element_type=F32)
        return carry

    lax.fori_loop(0, w_in.shape[0], step, 0)
    y = total[...].reshape(planes, C, 2 * lanes)
    a, b = y[:, :, :lanes], y[:, :, lanes:]
    return a + jnp.where(even_lanes(b.shape), behind(b, 1), ahead(b, 1))


def shot_step(x, weights, member, out_ref, part_ref, total):
    y = (x + net(x, *weights, total)).astype(BF16)
    out_ref[...] = y
    y = y.astype(F32)
    energy = jnp.sum(jnp.sum(y * y, axis=0), axis=0, keepdims=True)
    sums = jnp.sum(member[...] * energy, axis=1, keepdims=True)
    part_ref[...] = jnp.broadcast_to(sums, part_ref.shape)


def shifted(buf, lag_ref, shots, forward):
    planes, lanes = buf.shape[1] // 2, buf.shape[3]
    shape = (planes, C, lanes)
    even = even_lanes(shape)
    per = lanes // 2 // shots
    lane_shot = lax.rem(lax.broadcasted_iota(jnp.int32, shape, 2), lanes // 2) // per
    out = jnp.zeros(shape, F32)
    for s in range(shots):
        lag = lag_ref[s]
        half, odd = lag // 2, lax.rem(lag, 2)
        at_even = half if forward else planes - half - odd
        at_odd = half + odd if forward else planes - half
        one = jnp.where(even, buf[odd, pl.ds(at_even, planes)], buf[odd, pl.ds(at_odd, planes)])
        out = jnp.where(lane_shot == s, one, out)
    return out


def station_step(shots, sp, tot_ref, spread, weights, lags, join, mix, take, pace, buf, total):
    planes, _, lanes = sp.shape
    rows = planes * C
    mean = jnp.sum(tot_ref[:, 0:1] * spread[...], axis=0, keepdims=True)
    rms = jnp.sqrt(mean + EPSILON).reshape(1, 1, lanes)
    normed = (sp / rms).astype(BF16).astype(F32)
    settled = (sp + rms * net(normed, *weights, total)).astype(BF16).astype(F32)

    def fill(x, forward):
        far = ahead(x, planes) if forward else behind(x, planes)
        near_at, far_at = (0, planes) if forward else (planes, 0)
        for v, at in ((x, near_at), (far, far_at)):
            buf[0, at : at + planes] = v
            h = lanes // 2
            buf[1, at : at + planes] = jnp.concatenate([v[:, :, h:], v[:, :, :h]], axis=2)

    fill(settled, False)
    fired = shifted(buf, lags, shots, False).astype(BF16).reshape(rows, lanes)
    misfit = jnp.dot(fired, join[...], preferred_element_type=F32)
    misfit -= jnp.dot(mix[...], take[...], preferred_element_type=F32)
    fill(misfit.reshape(planes, C, lanes), True)
    return (settled - pace * shifted(buf, lags, shots, True)).astype(BF16)


def first_kernel(x, wi, wm, wo, bi, member, out, part, total):
    shot_step(x[...].astype(F32), (wi, wm, wo, bi), member, out, part, total)


def station_kernel(it, shots, lags, pace, sp, tot, spread, wi, wm, wo, bi, join, mix, take, out, buf, total):
    out[...] = station_step(
        shots, sp[...].astype(F32), tot, spread, (wi, wm, wo, bi), lags, join, mix, take, pace[it], buf, total
    )


def both_kernel(
    it, shots, lags, pace, sp, tot, spread, wi, wm, wo, bi, join, mix, take, vi, vm, vo, ci, member, out, part, buf, total
):
    x = station_step(
        shots, sp[...].astype(F32), tot, spread, (wi, wm, wo, bi), lags, join, mix, take, pace[it], buf, total
    )
    shot_step(x.astype(F32), (vi, vm, vo, ci), member, out, part, total)


def call(body, outs, ins, smem, scratch):
    v, s = pl.BlockSpec(memory_space=pltpu.VMEM), pl.BlockSpec(memory_space=pltpu.SMEM)
    return pl.pallas_call(
        body,
        out_shape=outs,
        in_specs=[s] * smem + [v] * (len(ins) - smem),
        out_specs=jax.tree.map(lambda _: v, outs),
        scratch_shapes=scratch,
        compiler_params=pltpu.CompilerParams(vmem_limit_bytes=48 * 2**20),
    )(*ins)


def prepared(w_in, w_mid, w_out, bias, near):
    n, feat = near.shape[1], w_in.shape[2]
    tiles = n // PACK
    near, own = near.astype(BF16), jnp.eye(n, dtype=BF16)
    w1 = jnp.stack([w_in[j] for j in TAPS])
    cols = near.reshape(3, n, tiles, PACK).transpose(0, 2, 1, 3)
    big = sum(w1[:, None, None, None, c, :] * cols[c][None, :, :, :, None] for c in range(3))
    big = big.transpose(1, 0, 2, 3, 4).reshape(tiles, 4 * n, PACK * feat)
    eye = jnp.eye(PACK, dtype=BF16)
    mid = (w_mid[:, None, :, None, :] * eye[None, :, None, :, None]).reshape(3 * PACK * feat, PACK * feat)
    w2 = jnp.stack([w_out[k] for k in TAPS])
    out = w2.T[None, None, :, :, None] * own.reshape(tiles, PACK, 1, 1, n)
    return big, mid, out.reshape(tiles, PACK * feat, 4 * n), jnp.tile(bias, (1, PACK))


def per_device(guess, mixtures, lags, order, tallies, e1, m1, x1, b1, e2, m2, x2, b2, pace):
    sh, recv, tl = guess.shape
    n_shot, n_line, n_tm = (lax.axis_size(a) for a in AXES)
    whole = RPL % (n_shot * n_line * n_tm) == 0
    where = AXES if whole else AXES[1:]
    parts = math.prod(lax.axis_size(a) for a in where)
    kp, lh = RPL // parts, recv // RPL
    lines, shots, nt = lh * n_line, sh * n_shot, tl * n_tm
    planes, s1 = nt // 2 // C, shots if whole else sh
    r1 = lines * kp
    r2 = r1 if whole else r1 // n_shot
    lanes1, lanes2 = 2 * s1 * r1, 2 * shots * r2
    sources = n_shot if whole else 1
    i32 = functools.partial(jnp.arange, dtype=jnp.int32)

    x = guess.reshape(sh, lh, parts, kp, tl).transpose(2, 0, 1, 3, 4)
    x = lax.all_to_all(x, where, split_axis=0, concat_axis=0)
    x = x.reshape(sources, n_line, n_tm, sh, lh, kp, tl).transpose(0, 3, 1, 4, 5, 2, 6)
    x = x.reshape(s1, r1, C, planes, 2).transpose(3, 2, 4, 0, 1).reshape(planes, C, lanes1)

    at_shot = lax.axis_index("shot")

    def first_k(line):
        block = line * n_tm + lax.axis_index("tm")
        return (at_shot * n_line * n_tm + block if whole else block) * kp

    n_mix = mixtures.shape[0]
    grid = mixtures.reshape(n_mix, lh, RPL, nt)
    sent = jnp.stack([lax.dynamic_slice_in_dim(grid, first_k(d), kp, axis=2) for d in range(n_line)])
    m = lax.all_to_all(sent, "line", split_axis=0, concat_axis=0)
    m = m.transpose(1, 0, 2, 3, 4).reshape(n_mix, r1, nt)
    if not whole:
        m = lax.dynamic_slice_in_dim(m, at_shot * r2, r2, axis=1)
    m = m.reshape(n_mix, r2, C, planes, 2).transpose(3, 2, 4, 0, 1).reshape(planes * C, 2 * n_mix * r2)

    np_ = tallies.shape[0]
    here = i32(np_)
    offsets = jnp.sum(jnp.where(here[None, :] < here[:, None], tallies[None, :], 0), axis=1)
    mine = first_k(lax.axis_index("line"))

    def one_hot(r):
        line, k = r // kp, mine + lax.rem(r, kp)
        q = lax.rem(line, lh) * RPL + k
        inside = (offsets[:, None] <= q[None, :]) & (q[None, :] < (offsets + tallies)[:, None])
        block = (line // lh)[None, :] == i32(n_line)[:, None]
        return (block[:, None, :] & inside[None, :, :]).reshape(n_line * np_, r.shape[0]).astype(F32)

    member = jnp.tile(one_hot(i32(r1)), (1, 2 * s1))
    r_own = i32(r2) if whole else at_shot * r2 + i32(r2)
    count = jnp.tile((tallies * (shots * nt)).astype(F32), n_line)
    spread = jnp.tile(one_hot(r_own) / count[:, None], (1, 2 * shots))

    sid = i32(shots)
    place = jnp.sum(jnp.where(order[None, :] == sid[:, None], sid[None, :], 0), axis=1)
    group = place // (shots // n_mix)
    same = (group[:, None] == group[None, :]).astype(BF16)
    chosen = (i32(n_mix)[:, None] == group[None, :]).astype(BF16)
    rest, two = jnp.eye(r2, dtype=BF16), jnp.eye(2, dtype=BF16)
    join = jnp.kron(two, jnp.kron(same, rest))
    take = jnp.kron(two, jnp.kron(chosen, rest))

    n1, n2 = s1 * r1, shots * r2
    a, b = i32(n1)[:, None], i32(n1)[None, :]
    near1 = jnp.stack([(a == b + (c - 1) * kp) & (a // r1 == b // r1) for c in range(3)])
    a, b = i32(n2)[:, None], i32(n2)[None, :]
    near2 = jnp.stack([a == b + (c - 1) * r2 for c in range(3)])
    wa = prepared(e1, m1, x1, b1, near1)
    wb = prepared(e2, m2, x2, b2, near2)

    rows = planes * C
    tot1, tot2 = pltpu.VMEM((rows, 2 * lanes1), F32), pltpu.VMEM((rows, 2 * lanes2), F32)
    buf = pltpu.VMEM((2, 2 * planes, C, lanes2), F32)
    spass = jax.ShapeDtypeStruct((planes, C, lanes1), BF16)
    part = jax.ShapeDtypeStruct((n_line * np_, 128), F32)
    moved = jax.ShapeDtypeStruct((planes, C, lanes2), BF16)

    def to_stations(y):
        y = y.reshape(rows, 2, sh, n_shot, r2)
        y = lax.all_to_all(y, "shot", split_axis=3, concat_axis=2, tiled=True)
        return y.reshape(planes, C, lanes2)

    def to_shots(y):
        y = y.reshape(rows, 2, shots, 1, r2)
        y = lax.all_to_all(y, "shot", split_axis=2, concat_axis=3, tiled=True)
        return y.reshape(planes, C, lanes1)

    sp, energy = call(first_kernel, (spass, part), (x, *wa, member), 0, [tot1])
    for it in range(ITERS):
        tot = lax.psum(energy, AXES)
        if not whole:
            sp = to_stations(sp)
        ins = (lags, pace, sp, tot, spread, *wb, join, m, take)
        if whole and it < ITERS - 1:
            sp, energy = call(
                functools.partial(both_kernel, it, shots), (spass, part), (*ins, *wa, member), 2, [buf, tot2]
            )
            continue
        x = call(functools.partial(station_kernel, it, shots), moved, ins, 2, [buf, tot2])
        if not whole:
            x = to_shots(x)
            if it < ITERS - 1:
                sp, energy = call(first_kernel, (spass, part), (x, *wa, member), 0, [tot1])

    x = x.reshape(planes, C, 2, s1, r1).transpose(3, 4, 1, 0, 2)
    x = x.reshape(sources, sh, n_line, lh, kp, n_tm, tl).transpose(0, 2, 5, 1, 3, 4, 6)
    x = lax.all_to_all(x.reshape(parts, sh, lh, kp, tl), where, split_axis=0, concat_axis=0)
    return x.transpose(1, 2, 0, 3, 4).reshape(sh, recv, tl)


def solution(mesh):
    spec = P(("group", "shot"), "line", "tm")
    placed = (spec, P("group", "line", None), P("group"), P("group"), P("group")) + (P(),) * 9
    return jax.shard_map(per_device, mesh=mesh, in_specs=placed, out_specs=spec, check_vma=False)
```

profile of v0, /device:TPU:0, one launch (start us, length us, event | category | flops | bytes accessed | tf_op | source)
XLA Modules:
  0.0 287.2 jit_solution(14768229795183627782)
XLA Ops:
  1.8 4.2 %all-to-all-start.1 = ((bf16[2,2,8,1,1024]{4,2,1,3,0:T(8,128)(2,1)}), bf16[2,2,8,1,1024]{4,2,1,3,0:T(8,128)(2,1)}, u32[]{:S(2)}, u32[]{:S(2)}) async-start(bf16[2,2,8,1,1024]{4,2,1,3,0:T(8,128)(2,1)} %pad_maximum_fusion), calls=%async_computation.1 | async-start | bytes 131072 | tf_op jit(solution)/shard_map/all_to_all | solution.py:190
  27.0 3.4 %mul.399 = bf16[16,4,64,4,64]{4,3,2,1,0:T(4,128)(2,1)} broadcast(bf16[16,64,4]{2,1,0:T(8,128)(2,1)S(1)} %copy.77), dimensions={0,2,3} | broadcast | bytes 2105344 | tf_op jit(solution)/shard_map/mul | solution.py:152
  30.4 6.0 %mul.400 = bf16[16,256,256]{2,1,0:T(8,128)(2,1)S(1)} reshape(bf16[16,4,64,4,64]{4,3,2,1,0:T(4,128)(2,1)} %mul.399) | data formatting | bytes 4194304 | tf_op jit(solution)/shard_map/mul | solution.py:152
  36.3 3.4 %mul.407 = bf16[16,4,64,4,64]{4,3,2,1,0:T(4,128)(2,1)} broadcast(bf16[16,64,4]{2,1,0:T(8,128)(2,1)S(1)} %copy.78), dimensions={0,2,3} | broadcast | bytes 2105344 | tf_op jit(solution)/shard_map/mul | solution.py:152
  39.7 7.0 %mul.408 = bf16[16,256,256]{2,1,0:T(8,128)(2,1)} reshape(bf16[16,4,64,4,64]{4,3,2,1,0:T(4,128)(2,1)} %mul.407) | data formatting | bytes 4194304 | tf_op jit(solution)/shard_map/mul | solution.py:152
  46.7 3.4 %mul.361 = bf16[16,4,64,4,64]{4,3,2,1,0:T(4,128)(2,1)} broadcast(bf16[16,64,4]{2,1,0:T(8,128)(2,1)S(1)} %copy.71), dimensions={0,2,3} | broadcast | bytes 2105344 | tf_op jit(solution)/shard_map/mul | solution.py:152
  50.1 7.0 %mul.362 = bf16[16,256,256]{2,1,0:T(8,128)(2,1)} reshape(bf16[16,4,64,4,64]{4,3,2,1,0:T(4,128)(2,1)} %mul.361) | data formatting | bytes 4194304 | tf_op jit(solution)/shard_map/mul | solution.py:152
  57.0 3.4 %mul.369 = bf16[16,4,64,4,64]{4,3,2,1,0:T(4,128)(2,1)} broadcast(bf16[16,64,4]{2,1,0:T(8,128)(2,1)S(1)} %copy.72), dimensions={0,2,3} | broadcast | bytes 2105344 | tf_op jit(solution)/shard_map/mul | solution.py:152
  60.4 7.0 %mul.370 = bf16[16,256,256]{2,1,0:T(8,128)(2,1)} reshape(bf16[16,4,64,4,64]{4,3,2,1,0:T(4,128)(2,1)} %mul.369) | data formatting | bytes 4194304 | tf_op jit(solution)/shard_map/mul | solution.py:152
  67.4 3.4 %mul.391 = bf16[16,4,64,4,64]{4,3,2,1,0:T(4,128)(2,1)} broadcast(bf16[16,64,4]{2,1,0:T(8,128)(2,1)S(1)} %copy.76), dimensions={0,2,3} | broadcast | bytes 2105344 | tf_op jit(solution)/shard_map/mul | solution.py:152
  70.8 7.0 %mul.392 = bf16[16,256,256]{2,1,0:T(8,128)(2,1)} reshape(bf16[16,4,64,4,64]{4,3,2,1,0:T(4,128)(2,1)} %mul.391) | data formatting | bytes 4194304 | tf_op jit(solution)/shard_map/mul | solution.py:152
  77.7 3.4 %mul.353 = bf16[16,4,64,4,64]{4,3,2,1,0:T(4,128)(2,1)} broadcast(bf16[16,64,4]{2,1,0:T(8,128)(2,1)S(1)} %copy.70), dimensions={0,2,3} | broadcast | bytes 2105344 | tf_op jit(solution)/shard_map/mul | solution.py:152
  81.2 7.1 %mul.354 = bf16[16,256,256]{2,1,0:T(8,128)(2,1)} reshape(bf16[16,4,64,4,64]{4,3,2,1,0:T(4,128)(2,1)} %mul.353) | data formatting | bytes 4194304 | tf_op jit(solution)/shard_map/mul | solution.py:152
  90.4 4.4 %multiply_add_fusion.wi = bf16[16,256,256]{2,1,0:T(8,128)(2,1)} fusion(bf16[16,256,256]{2,1,0:T(8,128)(2,1)} %mul.408, bf16[16,256,256]{2,1,0:T(8,128)(2,1)S(1)} %mul.400, bf16[16,256,256]{2,1,0:T(8,128)(2,1)} %mul.392, bf16[256,256]{1,0:T(8,128)(2,1)S(1)} %copy-done.11, bf16[256,256]{1,0:T(8,128)(2,1)S(1)} %copy-done.13, bf16[256,256]{1,0:T(8,128)(2,1)S(1)} %mul.388), kind=kLoop, calls=%fused_computation | loop fusion | flops 5242880 | bytes 8781824 | tf_op jit(solution)/shard_map/add | solution.py:152
  95.0 2.2 multiply_add_fusion.1.wi.vi
  100.5 3.0 %mul.379 = bf16[16,4,64,4,64]{4,3,2,1,0:T(4,128)(2,1)} broadcast(bf16[16,4,64]{2,1,0:T(4,128)(2,1)S(1)} %fusion.2), dimensions={0,1,4} | broadcast | bytes 2105344 | tf_op jit(solution)/shard_map/mul | solution.py:157
  103.6 7.0 %mul.380 = bf16[16,256,256]{2,1,0:T(8,128)(2,1)} reshape(bf16[16,4,64,4,64]{4,3,2,1,0:T(4,128)(2,1)} %mul.379) | data formatting | bytes 4194304 | tf_op jit(solution)/shard_map/mul | solution.py:157
  110.5 7.6 %all-to-all-start = ((bf16[16,1,8,1,512]{4,2,3,1,0:T(8,128)(2,1)}), bf16[16,1,8,1,512]{4,2,3,1,0:T(8,128)(2,1)}, u32[]{:S(2)}, u32[]{:S(2)}) async-start(bf16[16,1,8,1,512]{4,2,3,1,0:T(8,128)(2,1)} %copy.67), calls=%async_computation | async-start | bytes 262144 | tf_op jit(solution)/shard_map/all_to_all | solution.py:177
  118.2 3.3 %broadcast_multiply_fusion = (bf16[16,256,256]{2,1,0:T(8,128)(2,1)S(1)}, bf16[16,256,256]{2,1,0:T(8,128)(2,1)}) fusion(bf16[16,256,256]{2,1,0:T(8,128)(2,1)} %mul.380, bf16[256,256]{1,0:T(8,128)(2,1)S(1)} %mul.414, bf16[256,256]{1,0:T(8,128)(2,1)S(1)} %mul.377), kind=kLoop, calls=%fused_computation.2 | loop fusion | flops 2097152 | bytes 6553600 | tf_op jit(solution)/shard_map/mul | solution.py:157
  121.5 3.2 %copy.80 = bf16[2,2,8,1,1024]{2,1,4,0,3:T(2,128)(2,1)} copy(bf16[2,2,8,1,1024]{4,2,0,3,1:T(8,128)(2,1)} %bitcast.24) | data formatting | bytes 131072 | tf_op jit(solution)/shard_map/transpose | solution.py:191
  124.6 3.1 %reshape_reshape.3 = bf16[2,16,8,64,2]{1,4,3,2,0:T(2,128)(2,1)S(1)} reshape(bf16[2,2,8,1,1024]{2,1,4,0,3:T(2,128)(2,1)} %copy.80) | data formatting | bytes 131072 | tf_op jit(solution)/shard_map/reshape;reshape | solution.py:194
  127.7 1.6 copy.81
  130.7 5.0 %copy.68 = bf16[4,1,2,8,1,2,512]{3,2,6,5,0,4,1:T(2,128)(2,1)} copy(bf16[4,1,2,8,1,2,512]{6,3,5,2,0,4,1:T(8,128)(2,1)} %bitcast.3) | data formatting | bytes 262144 | tf_op jit(solution)/shard_map/transpose | solution.py:178
  135.8 5.7 %reshape.725 = bf16[4,16,8,64,2]{1,4,3,2,0:T(2,128)(2,1)} reshape(bf16[4,1,2,8,1,2,512]{3,2,6,5,0,4,1:T(2,128)(2,1)} %copy.68) | data formatting | bytes 262144 | tf_op jit(solution)/shard_map/reshape | solution.py:179
  141.5 3.4 %copy.69 = bf16[64,8,2,4,16]{0,4,3,2,1:T(8,128)(2,1)} copy(bf16[64,8,2,4,16]{4,2,0,1,3:T(2,128)(2,1)} %bitcast.68) | data formatting | bytes 262144 | tf_op jit(solution)/shard_map/transpose | solution.py:179
  147.6 1.6 copy-done.3
  149.2 13.0 %shard_map.136 = (bf16[64,8,128]{2,1,0:T(8,128)(2,1)S(1)}, f32[16,128]{1,0:T(8,128)S(1)}) custom-call(bf16[64,8,128]{2,1,0:T(8,128)(2,1)S(1)} %copy.75.x, bf16[16,256,256]{2,1,0:T(8,128)(2,1)S(1)} %copy-done.3, bf16[768,256]{1,0:T(8,128)(2,1)S(1)} %mul.375.wm.vm, bf16[16,256,256]{2,1,0:T(8,128)(2,1)S(1)} %copy-done, f32[2,256]{1,0:T(2,128)S(1)} %tile.19.bi.ci, ...), custom_call_target="tpu_custom_call" | custom-call | tf_op jit(solution)/shard_map/pallas_call | solution.py:136
  162.2 34.3 %psum.14.tot = f32[16,128]{1,0:T(8,128)S(1)} all-reduce(f32[16,128]{1,0:T(8,128)S(1)} %get-tuple-element.10), channel_id=1, replica_groups=mesh['group'=2,'shot'=4,'line'=2,'tm'=2] {'shot','line','tm'}, use_global_device_ids=true, to_apply=%region_1.2 | all-reduce | flops 2048 | bytes 16384 | tf_op jit(solution)/shard_map/psum | solution.py:249
  198.2 28.9 %shard_map.137 = (bf16[64,8,128]{2,1,0:T(8,128)(2,1)S(1)}, f32[16,128]{1,0:T(8,128)S(1)}) custom-call(s32[4]{0:T(128)S(1)} %copy-done.4, f32[2]{0:T(128)S(1)} %copy-done.5, bf16[64,8,128]{2,1,0:T(8,128)(2,1)S(1)} %get-tuple-element.9.sp, f32[16,128]{1,0:T(8,128)S(1)} %psum.14.tot, f32[16,128]{1,0:T(8,128)S(1)} %tile.48.spread, ...), custom_call_target="tpu_custom_call" | custom-call | tf_op jit(solution)/shard_map/pallas_call | solution.py:136
  227.1 30.0 %psum.15.tot = f32[16,128]{1,0:T(8,128)S(1)} all-reduce(f32[16,128]{1,0:T(8,128)S(1)} %get-tuple-element.12), channel_id=1, replica_groups=mesh['group'=2,'shot'=4,'line'=2,'tm'=2] {'shot','line','tm'}, use_global_device_ids=true, to_apply=%region_3.4 | all-reduce | flops 2048 | bytes 16384 | tf_op jit(solution)/shard_map/psum | solution.py:249
  258.7 14.2 %shard_map.138 = bf16[64,8,128]{2,1,0:T(8,128)(2,1)S(1)} custom-call(s32[4]{0:T(128)S(1)} %copy-done.4, f32[2]{0:T(128)S(1)} %copy-done.5, bf16[64,8,128]{2,1,0:T(8,128)(2,1)S(1)} %get-tuple-element.11.sp, f32[16,128]{1,0:T(8,128)S(1)} %psum.15.tot, f32[16,128]{1,0:T(8,128)S(1)} %tile.48.spread, bf16[16,256,256]{2,1,0:T(8,128)(2,1)S(1)} %copy-done.2, ...), custom_call_target="tpu_custom_call" | custom-call | tf_op jit(solution)/shard_map/pallas_call | solution.py:136
  276.0 10.5 %all_to_all.15 = bf16[16,1,8,1,512]{4,2,3,1,0:T(8,128)(2,1)S(1)} all-to-all(bf16[16,1,8,1,512]{4,2,3,1,0:T(8,128)(2,1)S(1)} %bitcast.72), channel_id=1, replica_groups=mesh['group'=2,'shot'=4,'line'=2,'tm'=2] {'shot','line','tm'}, dimensions={0} | all-to-all | bytes 262144 | tf_op jit(solution)/shard_map/all_to_all | solution.py:266
  (159 shorter events, 39.0 us)
Async XLA Ops:
  1.8 108.7 %all-to-all-start.1 = ((bf16[2,2,8,1,1024]{4,2,1,3,0:T(8,128)(2,1)}), bf16[2,2,8,1,1024]{4,2,1,3,0:T(8,128)(2,1)}, u32[]{:S(2)}, u32[]{:S(2)}) async-start(bf16[2,2,8,1,1024]{4,2,1,3,0:T(8,128)(2,1)} %pad_maximum_fusion), calls=%async_computation.1 | async-start | bytes 131072 | tf_op jit(solution)/shard_map/all_to_all | solution.py:190
  81.1 7.1 %copy-start.24 = (bf16[3,64]{1,0:T(4,128)(2,1)S(1)}, bf16[3,64]{1,0:T(4,128)(2,1)}, u32[]{:S(2)}) copy-start(bf16[3,64]{1,0:T(4,128)(2,1)} %slice.80) | copy-start | bytes 1156
  81.1 7.1 %copy-start.29 = (bf16[1,64]{1,0:T(2,128)(2,1)S(1)}, bf16[1,64]{1,0:T(2,128)(2,1)}, u32[]{:S(2)}) copy-start(bf16[1,64]{1,0:T(2,128)(2,1)} %slice.81) | copy-start | bytes 388
  81.1 7.7 %copy-start.18 = (bf16[3,64,64]{2,1,0:T(8,128)(2,1)S(1)}, bf16[3,64,64]{2,1,0:T(8,128)(2,1)}, u32[]{:S(2)}) copy-start(bf16[3,64,64]{2,1,0:T(8,128)(2,1)} %param.24) | copy-start | bytes 73732
  81.1 7.7 %copy-start.19 = (bf16[3,64,64]{2,1,0:T(8,128)(2,1)S(1)}, bf16[3,64,64]{2,1,0:T(8,128)(2,1)}, u32[]{:S(2)}) copy-start(bf16[3,64,64]{2,1,0:T(8,128)(2,1)} %param.20) | copy-start | bytes 73732
  81.1 7.7 %copy-start.27 = (bf16[4,4]{1,0:T(4,128)(2,1)S(1)}, bf16[4,4]{1,0:T(4,128)(2,1)}, u32[]{:S(2)}) copy-start(bf16[4,4]{1,0:T(4,128)(2,1)} %fusion.9) | copy-start | bytes 100
  81.1 9.2 %copy-start.11 = (bf16[256,256]{1,0:T(8,128)(2,1)S(1)}, bf16[256,256]{1,0:T(8,128)(2,1)}, u32[]{:S(2)}) copy-start(bf16[256,256]{1,0:T(8,128)(2,1)} %mul.404) | copy-start | bytes 393220
  81.1 9.2 %copy-start.13 = (bf16[256,256]{1,0:T(8,128)(2,1)S(1)}, bf16[256,256]{1,0:T(8,128)(2,1)}, u32[]{:S(2)}) copy-start(bf16[256,256]{1,0:T(8,128)(2,1)} %mul.396) | copy-start | bytes 393220
  90.4 4.5 %copy-start.6 = (bf16[16,256,256]{2,1,0:T(8,128)(2,1)S(1)}, bf16[16,256,256]{2,1,0:T(8,128)(2,1)}, u32[]{:S(2)}) copy-start(bf16[16,256,256]{2,1,0:T(8,128)(2,1)} %mul.362) | copy-start | bytes 6291460
  90.4 4.5 %copy-start.7 = (bf16[16,256,256]{2,1,0:T(8,128)(2,1)S(1)}, bf16[16,256,256]{2,1,0:T(8,128)(2,1)}, u32[]{:S(2)}) copy-start(bf16[16,256,256]{2,1,0:T(8,128)(2,1)} %mul.370) | copy-start | bytes 6291460
  90.4 4.5 %copy-start.8 = (bf16[16,256,256]{2,1,0:T(8,128)(2,1)S(1)}, bf16[16,256,256]{2,1,0:T(8,128)(2,1)}, u32[]{:S(2)}) copy-start(bf16[16,256,256]{2,1,0:T(8,128)(2,1)} %mul.354) | copy-start | bytes 6291460
  90.4 4.5 %copy-start.10 = (bf16[256,256]{1,0:T(8,128)(2,1)S(1)}, bf16[256,256]{1,0:T(8,128)(2,1)}, u32[]{:S(2)}) copy-start(bf16[256,256]{1,0:T(8,128)(2,1)} %mul.350) | copy-start | bytes 393220
  90.4 4.5 %copy-start.12 = (bf16[256,256]{1,0:T(8,128)(2,1)S(1)}, bf16[256,256]{1,0:T(8,128)(2,1)}, u32[]{:S(2)}) copy-start(bf16[256,256]{1,0:T(8,128)(2,1)} %mul.366) | copy-start | bytes 393220
  90.4 4.5 %copy-start.14 = (bf16[256,256]{1,0:T(8,128)(2,1)S(1)}, bf16[256,256]{1,0:T(8,128)(2,1)}, u32[]{:S(2)}) copy-start(bf16[256,256]{1,0:T(8,128)(2,1)} %mul.358) | copy-start | bytes 393220
  94.9 2.3 copy-start.23
  94.9 2.3 copy-start.28
  94.9 2.3 copy-start.25
  94.9 2.4 copy-start.26
  95.0 2.6 copy-start.22
  95.0 2.7 copy-start.17
  95.0 2.8 copy-start.21
  95.0 2.9 %copy-start.20 = (f32[16,16]{1,0:T(8,128)S(1)}, f32[16,16]{1,0:T(8,128)}, u32[]{:S(2)}) copy-start(f32[16,16]{1,0:T(8,128)} %broadcast_divide_fusion) | copy-start | bytes 3076
  95.0 3.0 %copy-start.15 = (bf16[2,64,2,64]{3,2,1,0:T(2,128)(2,1)S(1)}, bf16[2,64,2,64]{3,2,1,0:T(2,128)(2,1)}, u32[]{:S(2)}) copy-start(bf16[2,64,2,64]{3,2,1,0:T(2,128)(2,1)} %broadcast_multiply_fusion.4) | copy-start | bytes 98308
  95.0 3.1 %copy-start.16 = (bf16[1,128,512]{2,1,0:T(8,128)(2,1)S(1)}, bf16[1,128,512]{2,1,0:T(8,128)(2,1)}, u32[]{:S(2)}) copy-start(bf16[1,128,512]{2,1,0:T(8,128)(2,1)} %param.14) | copy-start | bytes 393220
  97.2 2.3 copy-start.9
  110.5 20.2 %all-to-all-start = ((bf16[16,1,8,1,512]{4,2,3,1,0:T(8,128)(2,1)}), bf16[16,1,8,1,512]{4,2,3,1,0:T(8,128)(2,1)}, u32[]{:S(2)}, u32[]{:S(2)}) async-start(bf16[16,1,8,1,512]{4,2,3,1,0:T(8,128)(2,1)} %copy.67), calls=%async_computation | async-start | bytes 262144 | tf_op jit(solution)/shard_map/all_to_all | solution.py:177
  146.0 1.6 copy-start
  147.6 1.6 copy-start.3
  149.2 47.4 %copy-start.4 = (s32[4]{0:T(128)S(1)}, s32[4]{0:T(128)}, u32[]{:S(2)}) copy-start(s32[4]{0:T(128)} %lags.3) | copy-start | bytes 52
  149.2 47.4 %copy-start.5 = (f32[2]{0:T(128)S(1)}, f32[2]{0:T(128)}, u32[]{:S(2)}) copy-start(f32[2]{0:T(128)} %pace.3) | copy-start | bytes 28
  196.6 1.6 copy-start.1
  257.1 1.6 copy-start.2
where the time goes:
time: 290 us; the launch traced here: 287 us
  local copies, waits for them, and re-layouts  125 us (43%)
  blocking collectives  74.8 us (26%)
  Pallas kernels  56.2 us (19%)
  other arithmetic  19 us (7%)
  starting transfers between devices  11.8 us (4%)
    mul x32, local copies, waits for them, and re-layouts, prepared(): w1[:, None, None, None, c, :] * cols[c][None, :, :, :, None]  67.6 us
    psum x2, blocking collectives, per_device(): tot = lax.psum(energy, AXES)  64.3 us
    pallas_call x3, Pallas kernels, call(): pl.pallas_call(body, out_shape=outs, in_specs=[s] * smem + [v] * (len(ins...  56.2 us
    mul x6, local copies, waits for them, and re-layouts, prepared(): out = w2.T[None, None, :, :, None] * own.reshape(tiles, PACK, 1, 1, n)  10.7 us
    all_to_all x1, blocking collectives, per_device(): lax.all_to_all(x.reshape(parts, sh, lh, kp, tl), where, split_axis=0, con...  10.5 us
    all_to_all x1, starting transfers between devices, per_device(): x = lax.all_to_all(x, where, split_axis=0, concat_axis=0)  7.64 us
    reshape x2, local copies, waits for them, and re-layouts, per_device(): x.reshape(s1, r1, C, planes, 2).transpose(3, 2, 4, 0, 1)  6.82 us
    add x2, other arithmetic, prepared(): sum((w1[:, None, None, None, c, :] * cols[c][None, :, :, :, None] for c i...  6.65 us
  transfers between devices with their start and end apart: 2, of which 0 were waited for; matrix products, arithmetic and copies ran while one was open for 41% of the time, Pallas kernels for 0%

commit v1 on v0

--- a/solution.py
+++ b/solution.py
@@ -3,6 +3,7 @@
 
 import jax
 import jax.numpy as jnp
+import numpy as np
 from jax import lax
 from jax.experimental import pallas as pl
 from jax.experimental.pallas import tpu as pltpu
@@ -34,16 +35,25 @@
     return lax.broadcasted_iota(jnp.int32, shape, len(shape) - 1) < shape[-1] // 2
 
 
-def net(x, w_in, w_mid, w_out, bias, total):
+def net(x, w_in, pick, w_mid, w_out, place, bias, total, band):
     planes, _, lanes = x.shape
     rows = planes * C
     side = jnp.where(even_lanes(x.shape), ahead(x, 1), behind(x, 1))
     z = jnp.concatenate([x, side], axis=2).astype(BF16).reshape(rows, 2 * lanes)
     total[...] = jnp.zeros_like(total)
-    wide = w_in.shape[2]
+    wide = w_in.shape[1]
+    feat = wide // PACK
+    for j in range(3):
+        tap = w_mid[j].astype(F32)
+        for i in range(PACK):
+            row = [tap if p == i else jnp.zeros_like(tap) for p in range(PACK)]
+            at = (j * PACK + i) * feat
+            band[at : at + feat, :] = jnp.concatenate(row, axis=1).astype(BF16)
 
     def step(q, carry):
-        h = jnp.dot(z, w_in[q], preferred_element_type=F32)
+        w_here = jnp.dot(pick[q], w_in[...], preferred_element_type=F32).astype(BF16)
+        o_here = jnp.dot(w_out[...], place[q], preferred_element_type=F32).astype(BF16)
+        h = jnp.dot(z, w_here, preferred_element_type=F32)
         h = jnp.maximum(h + bias[0:1, :], 0.0)
         cube = h.reshape(planes, C, wide)
         first = ahead(cube[:2], 2).reshape(2 * C, wide).astype(BF16)
@@ -51,19 +61,19 @@
         hb = h.astype(BF16)
         early = jnp.concatenate([last, hb[: rows - 2 * C]], axis=0)
         late = jnp.concatenate([hb[2 * C :], first], axis=0)
-        g = jnp.dot(jnp.concatenate([early, hb, late], axis=1), w_mid[...], preferred_element_type=F32)
+        g = jnp.dot(jnp.concatenate([early, hb, late], axis=1), band[...], preferred_element_type=F32)
         g = jnp.maximum(g + bias[1:2, :], 0.0).astype(BF16)
-        total[...] += jnp.dot(g, w_out[q], preferred_element_type=F32)
+        total[...] += jnp.dot(g, o_here, preferred_element_type=F32)
         return carry
 
-    lax.fori_loop(0, w_in.shape[0], step, 0)
+    lax.fori_loop(0, pick.shape[0], step, 0)
     y = total[...].reshape(planes, C, 2 * lanes)
     a, b = y[:, :, :lanes], y[:, :, lanes:]
     return a + jnp.where(even_lanes(b.shape), behind(b, 1), ahead(b, 1))
 
 
-def shot_step(x, weights, member, out_ref, part_ref, total):
-    y = (x + net(x, *weights, total)).astype(BF16)
+def shot_step(x, weights, member, out_ref, part_ref, total, band):
+    y = (x + net(x, *weights, total, band)).astype(BF16)
     out_ref[...] = y
     y = y.astype(F32)
     energy = jnp.sum(jnp.sum(y * y, axis=0), axis=0, keepdims=True)
@@ -88,13 +98,13 @@
     return out
 
 
-def station_step(shots, sp, tot_ref, spread, weights, lags, join, mix, take, pace, buf, total):
+def station_step(shots, sp, tot_ref, spread, weights, lags, join, mix, take, pace, buf, total, band):
     planes, _, lanes = sp.shape
     rows = planes * C
     mean = jnp.sum(tot_ref[:, 0:1] * spread[...], axis=0, keepdims=True)
     rms = jnp.sqrt(mean + EPSILON).reshape(1, 1, lanes)
     normed = (sp / rms).astype(BF16).astype(F32)
-    settled = (sp + rms * net(normed, *weights, total)).astype(BF16).astype(F32)
+    settled = (sp + rms * net(normed, *weights, total, band)).astype(BF16).astype(F32)
 
     def fill(x, forward):
         far = ahead(x, planes) if forward else behind(x, planes)
@@ -112,23 +122,23 @@
     return (settled - pace * shifted(buf, lags, shots, True)).astype(BF16)
 
 
-def first_kernel(x, wi, wm, wo, bi, member, out, part, total):
-    shot_step(x[...].astype(F32), (wi, wm, wo, bi), member, out, part, total)
-
-
-def station_kernel(it, shots, lags, pace, sp, tot, spread, wi, wm, wo, bi, join, mix, take, out, buf, total):
+def first_kernel(x, wi, wp, wm, wo, wq, bi, member, out, part, total, band):
+    shot_step(x[...].astype(F32), (wi, wp, wm, wo, wq, bi), member, out, part, total, band)
+
+
+def station_kernel(it, shots, lags, pace, sp, tot, spread, wi, wp, wm, wo, wq, bi, join, mix, take, out, buf, total, band):
     out[...] = station_step(
-        shots, sp[...].astype(F32), tot, spread, (wi, wm, wo, bi), lags, join, mix, take, pace[it], buf, total
+        shots, sp[...].astype(F32), tot, spread, (wi, wp, wm, wo, wq, bi), lags, join, mix, take, pace[it], buf, total, band
     )
 
 
 def both_kernel(
-    it, shots, lags, pace, sp, tot, spread, wi, wm, wo, bi, join, mix, take, vi, vm, vo, ci, member, out, part, buf, total
+    it, shots, lags, pace, sp, tot, spread, wi, wp, wm, wo, wq, bi, join, mix, take, vi, vp, vm, vo, vq, ci, member, out, part, buf, total, band
 ):
     x = station_step(
-        shots, sp[...].astype(F32), tot, spread, (wi, wm, wo, bi), lags, join, mix, take, pace[it], buf, total
+        shots, sp[...].astype(F32), tot, spread, (wi, wp, wm, wo, wq, bi), lags, join, mix, take, pace[it], buf, total, band
     )
-    shot_step(x.astype(F32), (vi, vm, vo, ci), member, out, part, total)
+    shot_step(x.astype(F32), (vi, vp, vm, vo, vq, ci), member, out, part, total, band)
 
 
 def call(body, outs, ins, smem, scratch):
@@ -146,16 +156,66 @@
 def prepared(w_in, w_mid, w_out, bias, near):
     n, feat = near.shape[1], w_in.shape[2]
     tiles = n // PACK
-    near, own = near.astype(BF16), jnp.eye(n, dtype=BF16)
-    w1 = jnp.stack([w_in[j] for j in TAPS])
-    cols = near.reshape(3, n, tiles, PACK).transpose(0, 2, 1, 3)
-    big = sum(w1[:, None, None, None, c, :] * cols[c][None, :, :, :, None] for c in range(3))
-    big = big.transpose(1, 0, 2, 3, 4).reshape(tiles, 4 * n, PACK * feat)
+    cols = near.reshape(3, n, tiles, PACK).transpose(2, 1, 0, 3)
+    pick = np.einsum("jk,tnci->tjnkci", np.eye(4), cols).reshape(tiles, 4 * n, 12 * PACK)
+    place = np.einsum("jk,tin->tjikn", np.eye(4), np.eye(n).reshape(tiles, PACK, n)).reshape(tiles, 4 * PACK, 4 * n)
+    w1 = jnp.stack([w_in[j] for j in TAPS]).reshape(12, 1, 1, feat)
     eye = jnp.eye(PACK, dtype=BF16)
-    mid = (w_mid[:, None, :, None, :] * eye[None, :, None, :, None]).reshape(3 * PACK * feat, PACK * feat)
-    w2 = jnp.stack([w_out[k] for k in TAPS])
-    out = w2.T[None, None, :, :, None] * own.reshape(tiles, PACK, 1, 1, n)
-    return big, mid, out.reshape(tiles, PACK * feat, 4 * n), jnp.tile(bias, (1, PACK))
+    rows = (w1 * eye[None, :, :, None]).reshape(12 * PACK, PACK * feat)
+    w2 = jnp.stack([w_out[k] for k in TAPS]).T.reshape(1, feat, 4, 1)
+    ends = (w2 * eye[:, None, None, :]).reshape(PACK * feat, 4 * PACK)
+    return rows, jnp.asarray(pick, BF16), w_mid, ends, jnp.asarray(place, BF16), jnp.tile(bias, (1, PACK))
+
+
+def exchange_kernel(sizes, x, out, slots, send, recv):
+    count = math.prod(sizes)
+    me = (lax.axis_index("shot") * sizes[1] + lax.axis_index("line")) * sizes[2] + lax.axis_index("tm")
+
+    def peer(off):
+        at = lax.rem(me + off, count)
+        return {
+            "shot": at // (sizes[1] * sizes[2]),
+            "line": lax.rem(at // sizes[2], sizes[1]),
+            "tm": lax.rem(at, sizes[2]),
+        }
+
+    barrier = pltpu.get_barrier_semaphore()
+    for off in range(1, count):
+        pl.semaphore_signal(barrier, inc=1, device_id=peer(off), device_id_type=pl.DeviceIdType.MESH)
+    pl.semaphore_wait(barrier, count - 1)
+    copies = []
+    for off in range(1, count):
+        copy = pltpu.make_async_remote_copy(
+            src_ref=x,
+            dst_ref=slots.at[off],
+            send_sem=send.at[off],
+            recv_sem=recv.at[off],
+            device_id=peer(off),
+            device_id_type=pl.DeviceIdType.MESH,
+        )
+        copy.start()
+        copies.append(copy)
+    total = x[...]
+    for off, copy in enumerate(copies, 1):
+        copy.wait()
+        total += slots[off]
+    out[...] = total
+
+
+def summed(x, sizes):
+    count, v = math.prod(sizes), pl.BlockSpec(memory_space=pltpu.VMEM)
+    return pl.pallas_call(
+        functools.partial(exchange_kernel, sizes),
+        out_shape=jax.ShapeDtypeStruct(x.shape, x.dtype),
+        in_specs=[v],
+        out_specs=v,
+        scratch_shapes=[
+            pltpu.VMEM((count, *x.shape), x.dtype),
+            pltpu.SemaphoreType.DMA((count,)),
+            pltpu.SemaphoreType.DMA((count,)),
+        ],
+        compiler_params=pltpu.CompilerParams(collective_id=0, has_side_effects=True),
+    )(x)
 
 
 def per_device(guess, mixtures, lags, order, tallies, e1, m1, x1, b1, e2, m2, x2, b2, pace):
@@ -220,15 +280,17 @@
     take = jnp.kron(two, jnp.kron(chosen, rest))
 
     n1, n2 = s1 * r1, shots * r2
-    a, b = i32(n1)[:, None], i32(n1)[None, :]
-    near1 = jnp.stack([(a == b + (c - 1) * kp) & (a // r1 == b // r1) for c in range(3)])
-    a, b = i32(n2)[:, None], i32(n2)[None, :]
-    near2 = jnp.stack([a == b + (c - 1) * r2 for c in range(3)])
+    a, b = np.arange(n1)[:, None], np.arange(n1)[None, :]
+    near1 = np.stack([(a == b + (c - 1) * kp) & (a // r1 == b // r1) for c in range(3)])
+    a, b = np.arange(n2)[:, None], np.arange(n2)[None, :]
+    near2 = np.stack([a == b + (c - 1) * r2 for c in range(3)])
     wa = prepared(e1, m1, x1, b1, near1)
     wb = prepared(e2, m2, x2, b2, near2)
 
     rows = planes * C
     tot1, tot2 = pltpu.VMEM((rows, 2 * lanes1), F32), pltpu.VMEM((rows, 2 * lanes2), F32)
+    feat = e1.shape[2]
+    band = pltpu.VMEM((3 * PACK * feat, PACK * feat), BF16)
     buf = pltpu.VMEM((2, 2 * planes, C, lanes2), F32)
     spass = jax.ShapeDtypeStruct((planes, C, lanes1), BF16)
     part = jax.ShapeDtypeStruct((n_line * np_, 128), F32)
@@ -244,22 +306,22 @@
         y = lax.all_to_all(y, "shot", split_axis=2, concat_axis=3, tiled=True)
         return y.reshape(planes, C, lanes1)
 
-    sp, energy = call(first_kernel, (spass, part), (x, *wa, member), 0, [tot1])
+    sp, energy = call(first_kernel, (spass, part), (x, *wa, member), 0, [tot1, band])
     for it in range(ITERS):
-        tot = lax.psum(energy, AXES)
+        tot = summed(energy, (n_shot, n_line, n_tm)) if whole else lax.psum(energy, AXES)
         if not whole:
             sp = to_stations(sp)
         ins = (lags, pace, sp, tot, spread, *wb, join, m, take)
         if whole and it < ITERS - 1:
             sp, energy = call(
-                functools.partial(both_kernel, it, shots), (spass, part), (*ins, *wa, member), 2, [buf, tot2]
+                functools.partial(both_kernel, it, shots), (spass, part), (*ins, *wa, member), 2, [buf, tot2, band]
             )
             continue
-        x = call(functools.partial(station_kernel, it, shots), moved, ins, 2, [buf, tot2])
+        x = call(functools.partial(station_kernel, it, shots), moved, ins, 2, [buf, tot2, band])
         if not whole:
             x = to_shots(x)
             if it < ITERS - 1:
-                sp, energy = call(first_kernel, (spass, part), (x, *wa, member), 0, [tot1])
+                sp, energy = call(first_kernel, (spass, part), (x, *wa, member), 0, [tot1, band])
 
     x = x.reshape(planes, C, 2, s1, r1).transpose(3, 4, 1, 0, 2)
     x = x.reshape(sources, sh, n_line, lh, kp, n_tm, tl).transpose(0, 2, 5, 1, 3, 4, 6)

time: 290 us -> 149 us (0.51)
  local copies, waits for them, and re-layouts: 125 us -> 31.5 us
  blocking collectives: 74.8 us -> 12.8 us
  Pallas kernels: 56.2 us -> 85.6 us
  other arithmetic: 19 us -> 3.75 us
  waiting for transfers between devices: 0.01 us -> 3.47 us
    mul x40 -> x8, local copies, waits for them, and re-layouts: 79.2 us -> 0.67 us  [the longest x4 0.42 us: prepared(): ends = (w2 * eye[:, None, None, :]).reshape(PACK * feat, 4 * PACK)]
    psum x2 -> x0, blocking collectives: 64.3 us -> none  [per_device(): tot = lax.psum(energy, AXES)]
    pallas_call x0 -> x2, Pallas kernels: none -> 16.2 us  [summed(): pl.pallas_call(functools.partial(exchange_kernel, sizes), out_shape=jax.S...]
    pallas_call x3, Pallas kernels: 56.2 us -> 69.4 us  [call(): pl.pallas_call(body, out_shape=outs, in_specs=[s] * smem + [v] * (len(ins...]
    add x6 -> x0, other arithmetic: 6.68 us -> none  [the longest x2 6.65 us: prepared(): sum((w1[:, None, None, None, c, :] * cols[c][None, :, :, :, None] for c i...]
    mul x4 -> x2, other arithmetic: 4.85 us -> 0.19 us  [the longest x1 0.11 us: prepared(): rows = (w1 * eye[None, :, :, None]).reshape(12 * PACK, PACK * feat)]
    unnamed x61 -> x25, local copies, waits for them, and re-layouts: 6.48 us -> 2.64 us
    all_to_all x1, waiting for transfers between devices: 0.01 us -> 3.47 us  [per_device(): x = lax.all_to_all(x, where, split_axis=0, concat_axis=0)]
  transfers between devices with their start and end apart: 2 -> 2, of which waited for: 0 -> 1; matrix products, arithmetic and copies ran while one was open for 41% -> 10% of each run, Pallas kernels for 0% -> 0%
where the time goes in v1:
time: 149 us
  Pallas kernels  85.6 us (57%)
  local copies, waits for them, and re-layouts  31.5 us (21%)
  blocking collectives  12.8 us (9%)
  starting transfers between devices  11.2 us (8%)
  other arithmetic  3.75 us (3%)
  waiting for transfers between devices  3.47 us (2%)
    pallas_call x3, Pallas kernels, call(): pl.pallas_call(body, out_shape=outs, in_specs=[s] * smem + [v] * (len(ins...  69.4 us
    pallas_call x2, Pallas kernels, summed(): pl.pallas_call(functools.partial(exchange_kernel, sizes), out_shape=jax.S...  16.2 us
    all_to_all x1, blocking collectives, per_device(): lax.all_to_all(x.reshape(parts, sh, lh, kp, tl), where, split_axis=0, con...  12.8 us
    all_to_all x1, starting transfers between devices, per_device(): x = lax.all_to_all(x, where, split_axis=0, concat_axis=0)  6.97 us
    reshape x2, local copies, waits for them, and re-layouts, per_device(): x.reshape(s1, r1, C, planes, 2).transpose(3, 2, 4, 0, 1)  5.99 us
    all_to_all x1, starting transfers between devices, per_device(): m = lax.all_to_all(sent, 'line', split_axis=0, concat_axis=0)  4.21 us
    transpose x1, local copies, waits for them, and re-layouts, per_device(): x.reshape(sources, n_line, n_tm, sh, lh, kp, tl)  3.7 us
    all_to_all x1, waiting for transfers between devices, per_device(): x = lax.all_to_all(x, where, split_axis=0, concat_axis=0)  3.47 us
  transfers between devices with their start and end apart: 2, of which 1 were waited for; matrix products, arithmetic and copies ran while one was open for 10% of the time, Pallas kernels for 0%

profile of v1, /device:TPU:0, one launch (start us, length us, event | category | flops | bytes accessed | tf_op | source)
XLA Modules:
  0.0 148.6 jit_solution(6827135129359454598)
XLA Ops:
  0.0 1.2 constant_dynamic-slice_fusion
  1.9 4.2 %all-to-all-start.1 = ((bf16[2,2,8,1,1024]{4,2,1,3,0:T(8,128)(2,1)}), bf16[2,2,8,1,1024]{4,2,1,3,0:T(8,128)(2,1)S(1)}, u32[]{:S(2)}, u32[]{:S(2)}) async-start(bf16[2,2,8,1,1024]{4,2,1,3,0:T(8,128)(2,1)} %pad_maximum_fusion), calls=%async_computation.1 | async-start | bytes 131072 | tf_op jit(solution)/shard_map/all_to_all | solution.py:250
  6.1 0.7 slice.41
  6.8 0.7 slice.40
  7.5 0.7 slice.37
  8.1 0.7 slice.36
  9.5 0.7 slice.38
  10.2 0.7 slice.43
  10.9 0.7 slice.42
  11.6 0.8 select_reduce_fusion.1
  12.7 0.8 select_reduce_fusion
  15.0 1.6 %copy.84 = bf16[16,1,8,1,512]{4,2,3,1,0:T(8,128)(2,1)} copy(bf16[16,1,8,1,512]{4,0,2,3,1:T(8,128)(2,1)} %bitcast.51) | data formatting | bytes 262144 | tf_op jit(solution)/shard_map/transpose | solution.py:236
  16.6 7.0 %all-to-all-start = ((bf16[16,1,8,1,512]{4,2,3,1,0:T(8,128)(2,1)}), bf16[16,1,8,1,512]{4,2,3,1,0:T(8,128)(2,1)S(1)}, u32[]{:S(2)}, u32[]{:S(2)}) async-start(bf16[16,1,8,1,512]{4,2,3,1,0:T(8,128)(2,1)} %copy.84), calls=%async_computation | async-start | bytes 262144 | tf_op jit(solution)/shard_map/all_to_all | solution.py:237
  23.9 0.7 tile.18
  25.7 0.8 copy.92
  27.0 0.8 copy.93
  28.1 3.5 %all-to-all-done = bf16[16,1,8,1,512]{4,2,3,1,0:T(8,128)(2,1)S(1)} async-done(((bf16[16,1,8,1,512]{4,2,3,1,0:T(8,128)(2,1)}), bf16[16,1,8,1,512]{4,2,3,1,0:T(8,128)(2,1)S(1)}, u32[]{:S(2)}, u32[]{:S(2)}) %all-to-all-start) | async-done | bytes 131104 | tf_op jit(solution)/shard_map/all_to_all | solution.py:237
  31.5 3.7 %copy.85 = bf16[4,1,2,8,1,2,512]{3,2,6,5,0,4,1:T(2,128)(2,1)} copy(bf16[4,1,2,8,1,2,512]{6,3,5,2,0,4,1:T(8,128)(2,1)S(1)} %bitcast.48) | data formatting | bytes 262144 | tf_op jit(solution)/shard_map/transpose | solution.py:238
  35.2 5.8 %reshape.354 = bf16[4,16,8,64,2]{1,4,3,2,0:T(2,128)(2,1)} reshape(bf16[4,1,2,8,1,2,512]{3,2,6,5,0,4,1:T(2,128)(2,1)} %copy.85) | data formatting | bytes 262144 | tf_op jit(solution)/shard_map/reshape | solution.py:239
  41.1 2.5 %copy.86 = bf16[64,8,2,4,16]{0,4,3,2,1:T(8,128)(2,1)S(1)} copy(bf16[64,8,2,4,16]{4,2,0,1,3:T(2,128)(2,1)} %bitcast.44) | data formatting | bytes 262144 | tf_op jit(solution)/shard_map/transpose | solution.py:239
  43.8 16.9 %shard_map.172 = (bf16[64,8,128]{2,1,0:T(8,128)(2,1)S(1)}, f32[16,128]{1,0:T(8,128)S(1)}) custom-call(bf16[64,8,128]{2,1,0:T(8,128)(2,1)S(1)} %copy.89.x, bf16[48,256]{1,0:T(8,128)(2,1)S(1)} %mul.200.wi.vi, bf16[16,256,48]{2,1,0:T(8,128)(2,1)S(1)} %copy-done.1, bf16[3,64,64]{2,1,0:T(8,128)(2,1)S(1)} %copy-done.3, bf16[256,16]{1,0:T(8,128)(2,1)S(1)} %copy.90.wo.vo, ...), custom_call_target="tpu_custom_call" | custom-call | tf_op jit(solution)/shard_map/pallas_call | solution.py:146
  61.2 8.1 %shard_map.173.tot = f32[16,128]{1,0:T(8,128)} custom-call(f32[16,128]{1,0:T(8,128)} %copy-done.8), custom_call_target="tpu_custom_call" | custom-call | tf_op jit(solution)/shard_map/pallas_call | solution.py:207
  69.4 0.7 copy-done.6
  70.1 34.7 %shard_map.174 = (bf16[64,8,128]{2,1,0:T(8,128)(2,1)S(1)}, f32[16,128]{1,0:T(8,128)S(1)}) custom-call(s32[4]{0:T(128)S(1)} %copy-done.9, f32[2]{0:T(128)S(1)} %copy-done.10, bf16[64,8,128]{2,1,0:T(8,128)(2,1)S(1)} %get-tuple-element.9.sp, f32[16,128]{1,0:T(8,128)S(1)} %copy-done.6, f32[16,128]{1,0:T(8,128)S(1)} %tile.48.spread, ...), custom_call_target="tpu_custom_call" | custom-call | tf_op jit(solution)/shard_map/pallas_call | solution.py:146
  105.4 8.1 %shard_map.175.tot = f32[16,128]{1,0:T(8,128)} custom-call(f32[16,128]{1,0:T(8,128)} %copy-done.7), custom_call_target="tpu_custom_call" | custom-call | tf_op jit(solution)/shard_map/pallas_call | solution.py:207
  113.5 0.7 copy-done.5
  114.2 17.8 %shard_map.176 = bf16[64,8,128]{2,1,0:T(8,128)(2,1)S(1)} custom-call(s32[4]{0:T(128)S(1)} %copy-done.9, f32[2]{0:T(128)S(1)} %copy-done.10, bf16[64,8,128]{2,1,0:T(8,128)(2,1)S(1)} %get-tuple-element.11.sp, f32[16,128]{1,0:T(8,128)S(1)} %copy-done.5, f32[16,128]{1,0:T(8,128)S(1)} %tile.48.spread, bf16[48,256]{1,0:T(8,128)(2,1)S(1)} %mul.212.wi, ...), custom_call_target="tpu_custom_call" | custom-call | tf_op jit(solution)/shard_map/pallas_call | solution.py:146
  132.2 0.8 copy.98
  133.0 0.8 reshape.359
  133.8 1.2 copy.99
  135.1 12.8 %all_to_all.15 = bf16[16,1,8,1,512]{4,2,3,1,0:T(8,128)(2,1)S(1)} all-to-all(bf16[16,1,8,1,512]{4,2,3,1,0:T(8,128)(2,1)S(1)} %bitcast.49), channel_id=1, replica_groups=mesh['group'=2,'shot'=4,'line'=2,'tm'=2] {'shot','line','tm'}, dimensions={0} | all-to-all | bytes 262144 | tf_op jit(solution)/shard_map/all_to_all | solution.py:328
  147.9 0.7 copy.101
  (76 shorter events, 6.9 us)
Async XLA Ops:
  0.0 25.2 %copy-start.11 = (f32[2,64]{1,0:T(2,128)S(1)}, f32[2,64]{1,0:T(2,128)}, u32[]{:S(2)}) copy-start(f32[2,64]{1,0:T(2,128)} %param.30) | copy-start | bytes 1540
  1.9 14.8 %all-to-all-start.1 = ((bf16[2,2,8,1,1024]{4,2,1,3,0:T(8,128)(2,1)}), bf16[2,2,8,1,1024]{4,2,1,3,0:T(8,128)(2,1)S(1)}, u32[]{:S(2)}, u32[]{:S(2)}) async-start(bf16[2,2,8,1,1024]{4,2,1,3,0:T(8,128)(2,1)} %pad_maximum_fusion), calls=%async_computation.1 | async-start | bytes 131072 | tf_op jit(solution)/shard_map/all_to_all | solution.py:250
  16.6 14.9 %all-to-all-start = ((bf16[16,1,8,1,512]{4,2,3,1,0:T(8,128)(2,1)}), bf16[16,1,8,1,512]{4,2,3,1,0:T(8,128)(2,1)S(1)}, u32[]{:S(2)}, u32[]{:S(2)}) async-start(bf16[16,1,8,1,512]{4,2,3,1,0:T(8,128)(2,1)} %copy.84), calls=%async_computation | async-start | bytes 262144 | tf_op jit(solution)/shard_map/all_to_all | solution.py:237
  35.2 8.5 %copy-start.1 = (bf16[16,256,48]{2,1,0:T(8,128)(2,1)S(1)}, bf16[16,256,48]{2,1,0:T(8,128)(2,1)}, u32[]{:S(2)}) copy-start(bf16[16,256,48]{2,1,0:T(8,128)(2,1)} %constant.70.clone.wp.vp) | copy-start | bytes 1179652
  35.2 8.5 %copy-start.2 = (bf16[16,16,256]{2,1,0:T(8,128)(2,1)S(1)}, bf16[16,16,256]{2,1,0:T(8,128)(2,1)}, u32[]{:S(2)}) copy-start(bf16[16,16,256]{2,1,0:T(8,128)(2,1)} %constant.71.clone.wq.vq) | copy-start | bytes 393220
  35.2 8.5 %copy-start.3 = (bf16[3,64,64]{2,1,0:T(8,128)(2,1)S(1)}, bf16[3,64,64]{2,1,0:T(8,128)(2,1)}, u32[]{:S(2)}) copy-start(bf16[3,64,64]{2,1,0:T(8,128)(2,1)} %vm.1) | copy-start | bytes 73732
  41.1 28.3 %copy-start = (bf16[16,256,48]{2,1,0:T(8,128)(2,1)S(1)}, bf16[16,256,48]{2,1,0:T(8,128)(2,1)}, u32[]{:S(2)}) copy-start(bf16[16,256,48]{2,1,0:T(8,128)(2,1)} %constant.72.clone.wp) | copy-start | bytes 1179652
  41.1 28.3 %copy-start.4 = (bf16[3,64,64]{2,1,0:T(8,128)(2,1)S(1)}, bf16[3,64,64]{2,1,0:T(8,128)(2,1)}, u32[]{:S(2)}) copy-start(bf16[3,64,64]{2,1,0:T(8,128)(2,1)} %wm.5) | copy-start | bytes 73732
  41.1 28.3 %copy-start.9 = (s32[4]{0:T(128)S(1)}, s32[4]{0:T(128)}, u32[]{:S(2)}) copy-start(s32[4]{0:T(128)} %lags.3) | copy-start | bytes 52
  41.1 28.3 %copy-start.10 = (f32[2]{0:T(128)S(1)}, f32[2]{0:T(128)}, u32[]{:S(2)}) copy-start(f32[2]{0:T(128)} %pace.3) | copy-start | bytes 28
  60.6 0.6 copy-start.8
  69.4 0.7 copy-start.6
  104.7 0.6 copy-start.7
  113.5 0.7 copy-start.5

commit v2 on v1

--- a/solution.py
+++ b/solution.py
@@ -66,7 +66,7 @@
         total[...] += jnp.dot(g, o_here, preferred_element_type=F32)
         return carry
 
-    lax.fori_loop(0, pick.shape[0], step, 0)
+    lax.fori_loop(0, pick.shape[0], step, 0, unroll=2)
     y = total[...].reshape(planes, C, 2 * lanes)
     a, b = y[:, :, :lanes], y[:, :, lanes:]
     return a + jnp.where(even_lanes(b.shape), behind(b, 1), ahead(b, 1))
@@ -122,6 +122,63 @@
     return (settled - pace * shifted(buf, lags, shots, True)).astype(BF16)
 
 
+def by_phase(width):
+    row = lax.broadcasted_iota(jnp.int32, (width, width), 0)
+    col = lax.broadcasted_iota(jnp.int32, (width, width), 1)
+    half = width // 2
+    return jnp.where(col == 2 * lax.rem(row, half) + row // half, 1.0, 0.0).astype(BF16)
+
+
+def unfold(read, into, sort):
+    planes = into.shape[0]
+    for c in range(C):
+        v = lax.dot_general(sort, read(c), (((1,), (1,)), ((), ())), preferred_element_type=F32)
+        into[:, c, :] = jnp.concatenate([v[:planes], v[planes:]], axis=1)
+
+
+def entry_kernel(
+    dims, x, m, wi, wp, wm, wo, wq, bi, member, out, part, mix, total, band, cube, side
+):
+    shots, blocks, halves = dims
+    width = 2 * cube.shape[0]
+    sort, each = by_phase(width), C // halves
+
+    def traces(c):
+        at, t = slice(c % each * width, (c % each + 1) * width), c // each
+        rows = [x[(s * blocks + b) * halves + t, :, at].astype(F32) for s in range(shots) for b in range(blocks)]
+        return jnp.concatenate(rows, axis=0).astype(BF16)
+
+    def records(c):
+        at = slice(c * width, (c + 1) * width)
+        rows = [m[b, g, :, at].astype(F32) for g in range(m.shape[1]) for b in range(blocks)]
+        return jnp.concatenate(rows, axis=0).astype(BF16)
+
+    unfold(records, side, sort)
+    mix[...] = side[...].astype(BF16).reshape(mix.shape)
+    unfold(traces, cube, sort)
+    shot_step(cube[...], (wi, wp, wm, wo, wq, bi), member, out, part, total, band)
+
+
+def exit_kernel(
+    it, dims, lags, pace, sp, tot, spread, wi, wp, wm, wo, wq, bi, join, mix, take, out, buf, total, band, cube
+):
+    shots, blocks, halves = dims
+    width = 2 * cube.shape[0]
+    sort, each = by_phase(width), C // halves
+    x = station_step(
+        shots, sp[...].astype(F32), tot, spread, (wi, wp, wm, wo, wq, bi), lags, join, mix, take, pace[it], buf, total, band
+    )
+    cube[...] = x.astype(F32)
+    n, lh = cube.shape[2] // 2, out.shape[1]
+    for c in range(C):
+        v = cube[:, c, :]
+        v = jnp.concatenate([v[:, :n], v[:, n:]], axis=0).T.astype(BF16)
+        v = jnp.dot(v, sort, preferred_element_type=F32)
+        at, t = slice(c % each * width, (c % each + 1) * width), c // each
+        for j in range(shots * blocks):
+            out[j * halves + t, :, at] = v[j * lh : (j + 1) * lh].astype(BF16)
+
+
 def first_kernel(x, wi, wp, wm, wo, wq, bi, member, out, part, total, band):
     shot_step(x[...].astype(F32), (wi, wp, wm, wo, wq, bi), member, out, part, total, band)
 
@@ -157,12 +214,12 @@
     n, feat = near.shape[1], w_in.shape[2]
     tiles = n // PACK
     cols = near.reshape(3, n, tiles, PACK).transpose(2, 1, 0, 3)
-    pick = np.einsum("jk,tnci->tjnkci", np.eye(4), cols).reshape(tiles, 4 * n, 12 * PACK)
-    place = np.einsum("jk,tin->tjikn", np.eye(4), np.eye(n).reshape(tiles, PACK, n)).reshape(tiles, 4 * PACK, 4 * n)
-    w1 = jnp.stack([w_in[j] for j in TAPS]).reshape(12, 1, 1, feat)
+    pick = np.einsum("jk,tnci->tjnkci", np.eye(4)[list(TAPS)], cols).reshape(tiles, 4 * n, 12 * PACK)
+    place = np.einsum("kj,tin->tjikn", np.eye(4)[list(TAPS)], np.eye(n).reshape(tiles, PACK, n)).reshape(tiles, 4 * PACK, 4 * n)
+    w1 = w_in.reshape(12, 1, 1, feat)
     eye = jnp.eye(PACK, dtype=BF16)
     rows = (w1 * eye[None, :, :, None]).reshape(12 * PACK, PACK * feat)
-    w2 = jnp.stack([w_out[k] for k in TAPS]).T.reshape(1, feat, 4, 1)
+    w2 = w_out.T.reshape(1, feat, 4, 1)
     ends = (w2 * eye[:, None, None, :]).reshape(PACK * feat, 4 * PACK)
     return rows, jnp.asarray(pick, BF16), w_mid, ends, jnp.asarray(place, BF16), jnp.tile(bias, (1, PACK))
 
@@ -235,8 +292,12 @@
 
     x = guess.reshape(sh, lh, parts, kp, tl).transpose(2, 0, 1, 3, 4)
     x = lax.all_to_all(x, where, split_axis=0, concat_axis=0)
-    x = x.reshape(sources, n_line, n_tm, sh, lh, kp, tl).transpose(0, 3, 1, 4, 5, 2, 6)
-    x = x.reshape(s1, r1, C, planes, 2).transpose(3, 2, 4, 0, 1).reshape(planes, C, lanes1)
+    fused = whole and sh == 1 and kp == 1 and C % n_tm == 0
+    if fused:
+        x = x.reshape(parts, lh, tl)
+    else:
+        x = x.reshape(sources, n_line, n_tm, sh, lh, kp, tl).transpose(0, 3, 1, 4, 5, 2, 6)
+        x = x.reshape(s1, r1, C, planes, 2).transpose(3, 2, 4, 0, 1).reshape(planes, C, lanes1)
 
     at_shot = lax.axis_index("shot")
 
@@ -248,10 +309,13 @@
     grid = mixtures.reshape(n_mix, lh, RPL, nt)
     sent = jnp.stack([lax.dynamic_slice_in_dim(grid, first_k(d), kp, axis=2) for d in range(n_line)])
     m = lax.all_to_all(sent, "line", split_axis=0, concat_axis=0)
-    m = m.transpose(1, 0, 2, 3, 4).reshape(n_mix, r1, nt)
-    if not whole:
-        m = lax.dynamic_slice_in_dim(m, at_shot * r2, r2, axis=1)
-    m = m.reshape(n_mix, r2, C, planes, 2).transpose(3, 2, 4, 0, 1).reshape(planes * C, 2 * n_mix * r2)
+    if fused:
+        m = m.reshape(n_line, n_mix, lh, nt)
+    else:
+        m = m.transpose(1, 0, 2, 3, 4).reshape(n_mix, r1, nt)
+        if not whole:
+            m = lax.dynamic_slice_in_dim(m, at_shot * r2, r2, axis=1)
+        m = m.reshape(n_mix, r2, C, planes, 2).transpose(3, 2, 4, 0, 1).reshape(planes * C, 2 * n_mix * r2)
 
     np_ = tallies.shape[0]
     here = i32(np_)
@@ -306,7 +370,20 @@
         y = lax.all_to_all(y, "shot", split_axis=2, concat_axis=3, tiled=True)
         return y.reshape(planes, C, lanes1)
 
-    sp, energy = call(first_kernel, (spass, part), (x, *wa, member), 0, [tot1, band])
+    dims = (n_shot, n_line, n_tm)
+    cube = pltpu.VMEM((planes, C, lanes1), F32)
+    if fused:
+        mixed = jax.ShapeDtypeStruct((rows, 2 * n_mix * r2), BF16)
+        side = pltpu.VMEM((planes, C, 2 * n_mix * r2), F32)
+        sp, energy, m = call(
+            functools.partial(entry_kernel, dims),
+            (spass, part, mixed),
+            (x, m, *wa, member),
+            0,
+            [tot1, band, cube, side],
+        )
+    else:
+        sp, energy = call(first_kernel, (spass, part), (x, *wa, member), 0, [tot1, band])
     for it in range(ITERS):
         tot = summed(energy, (n_shot, n_line, n_tm)) if whole else lax.psum(energy, AXES)
         if not whole:
@@ -317,14 +394,19 @@
                 functools.partial(both_kernel, it, shots), (spass, part), (*ins, *wa, member), 2, [buf, tot2, band]
             )
             continue
+        if fused:
+            back = jax.ShapeDtypeStruct((parts, lh, tl), BF16)
+            x = call(functools.partial(exit_kernel, it, dims), back, ins, 2, [buf, tot2, band, cube])
+            continue
         x = call(functools.partial(station_kernel, it, shots), moved, ins, 2, [buf, tot2, band])
         if not whole:
             x = to_shots(x)
             if it < ITERS - 1:
                 sp, energy = call(first_kernel, (spass, part), (x, *wa, member), 0, [tot1, band])
 
-    x = x.reshape(planes, C, 2, s1, r1).transpose(3, 4, 1, 0, 2)
-    x = x.reshape(sources, sh, n_line, lh, kp, n_tm, tl).transpose(0, 2, 5, 1, 3, 4, 6)
+    if not fused:
+        x = x.reshape(planes, C, 2, s1, r1).transpose(3, 4, 1, 0, 2)
+        x = x.reshape(sources, sh, n_line, lh, kp, n_tm, tl).transpose(0, 2, 5, 1, 3, 4, 6)
     x = lax.all_to_all(x.reshape(parts, sh, lh, kp, tl), where, split_axis=0, concat_axis=0)
     return x.transpose(1, 2, 0, 3, 4).reshape(sh, recv, tl)
 

time: 149 us -> 126 us (0.85)
  local copies, waits for them, and re-layouts: 31.5 us -> 8.06 us
  waiting for transfers between devices: 3.47 us -> 7.9 us
  other arithmetic: 3.75 us -> 1.74 us
    transpose x6 -> x0, local copies, waits for them, and re-layouts: 9.74 us -> none  [the longest x1 3.7 us: per_device(): x.reshape(sources, n_line, n_tm, sh, lh, kp, tl)]
    reshape x4 -> x0, local copies, waits for them, and re-layouts: 7.12 us -> none  [the longest x2 5.99 us: per_device(): x.reshape(s1, r1, C, planes, 2).transpose(3, 2, 4, 0, 1)]
    slice x8 -> x0, local copies, waits for them, and re-layouts: 5.48 us -> none  [the longest x4 2.76 us: prepared(): w1 = jnp.stack([w_in[j] for j in TAPS]).reshape(12, 1, 1, feat)]
    all_to_all x1, waiting for transfers between devices: 3.47 us -> 5.96 us  [per_device(): x = lax.all_to_all(x, where, split_axis=0, concat_axis=0)]
    all_to_all x1, waiting for transfers between devices: 0.01 us -> 1.95 us  [per_device(): m = lax.all_to_all(sent, 'line', split_axis=0, concat_axis=0)]
    unnamed x25 -> x42, local copies, waits for them, and re-layouts: 2.64 us -> 3.85 us
  transfers between devices with their start and end apart: 2 -> 2, of which waited for: 1 -> 2; matrix products, arithmetic and copies ran while one was open for 10% -> 3% of each run, Pallas kernels for 0% -> 0%
where the time goes in v2:
time: 126 us; the launch traced here: 125 us
  Pallas kernels  84.5 us (67%)
  blocking collectives  12.8 us (10%)
  starting transfers between devices  9.85 us (8%)
  local copies, waits for them, and re-layouts  8.06 us (6%)
  waiting for transfers between devices  7.9 us (6%)
  other arithmetic  1.74 us (1%)
    pallas_call x3, Pallas kernels, call(): pl.pallas_call(body, out_shape=outs, in_specs=[s] * smem + [v] * (len(ins...  68.3 us
    pallas_call x2, Pallas kernels, summed(): pl.pallas_call(functools.partial(exchange_kernel, sizes), out_shape=jax.S...  16.2 us
    all_to_all x1, blocking collectives, per_device(): lax.all_to_all(x.reshape(parts, sh, lh, kp, tl), where, split_axis=0, con...  12.8 us
    all_to_all x1, waiting for transfers between devices, per_device(): x = lax.all_to_all(x, where, split_axis=0, concat_axis=0)  5.96 us
    all_to_all x1, starting transfers between devices, per_device(): x = lax.all_to_all(x, where, split_axis=0, concat_axis=0)  5.51 us
    all_to_all x1, starting transfers between devices, per_device(): m = lax.all_to_all(sent, 'line', split_axis=0, concat_axis=0)  4.34 us
    unnamed x42, local copies, waits for them, and re-layouts  3.85 us
  transfers between devices with their start and end apart: 2, of which 2 were waited for; matrix products, arithmetic and copies ran while one was open for 3% of the time, Pallas kernels for 0%

profile of v2, /device:TPU:0, one launch (start us, length us, event | category | flops | bytes accessed | tf_op | source)
XLA Modules:
  0.0 125.2 jit_solution(12782403267850926843)
XLA Ops:
  0.0 1.2 constant_dynamic-slice_fusion.1
  1.3 0.6 pad_maximum_fusion
  1.9 4.3 %all-to-all-start.1 = ((bf16[2,2,8,1,1024]{4,2,1,3,0:T(8,128)(2,1)}), bf16[2,2,8,1,1024]{4,2,1,3,0:T(8,128)(2,1)S(1)}, u32[]{:S(2)}, u32[]{:S(2)}) async-start(bf16[2,2,8,1,1024]{4,2,1,3,0:T(8,128)(2,1)} %pad_maximum_fusion), calls=%async_computation.1 | async-start | bytes 131072 | tf_op jit(solution)/shard_map/all_to_all | solution.py:311
  6.3 0.1 select_reduce_fusion.1
  6.5 0.1 select_reduce_fusion
  6.7 0.1 copy.50
  7.0 0.1 mul.220
  7.4 0.1 broadcast_multiply_fusion
  7.5 0.1 broadcast_multiply_fusion.2
  7.7 0.7 copy.46
  8.4 1.9 %all-to-all-done.1 = bf16[2,2,8,1,1024]{4,2,1,3,0:T(8,128)(2,1)S(1)} async-done(((bf16[2,2,8,1,1024]{4,2,1,3,0:T(8,128)(2,1)}), bf16[2,2,8,1,1024]{4,2,1,3,0:T(8,128)(2,1)S(1)}, u32[]{:S(2)}, u32[]{:S(2)}) %all-to-all-start.1) | async-done | bytes 65568 | tf_op jit(solution)/shard_map/all_to_all | solution.py:311
  10.4 5.5 %all-to-all-start = ((bf16[16,1,8,1,512]{4,2,3,1,0:T(8,128)(2,1)}), bf16[16,1,8,1,512]{4,2,3,1,0:T(8,128)(2,1)S(1)}, u32[]{:S(2)}, u32[]{:S(2)}) async-start(bf16[16,1,8,1,512]{4,2,3,1,0:T(8,128)(2,1)} %copy.46), calls=%async_computation | async-start | bytes 262144 | tf_op jit(solution)/shard_map/all_to_all | solution.py:294
  16.0 0.1 mul.201.wi.vi
  16.2 0.1 copy.51.wo.vo
  16.3 0.5 copy-done.16
  17.1 0.1 mul.223.join
  17.3 0.1 broadcast_multiply_fusion.4
  17.5 0.1 mul.212.wi
  17.6 0.1 copy.53.wo
  17.9 6.0 %all-to-all-done = bf16[16,1,8,1,512]{4,2,3,1,0:T(8,128)(2,1)S(1)} async-done(((bf16[16,1,8,1,512]{4,2,3,1,0:T(8,128)(2,1)}), bf16[16,1,8,1,512]{4,2,3,1,0:T(8,128)(2,1)S(1)}, u32[]{:S(2)}, u32[]{:S(2)}) %all-to-all-start) | async-done | bytes 131104 | tf_op jit(solution)/shard_map/all_to_all | solution.py:294
  23.9 16.8 %shard_map.172 = (bf16[64,8,128]{2,1,0:T(8,128)(2,1)S(1)}, f32[16,128]{1,0:T(8,128)S(1)}, bf16[512,64]{1,0:T(8,128)(2,1)S(1)}) custom-call(bf16[16,8,512]{2,1,0:T(8,128)(2,1)S(1)} %bitcast.26, bf16[2,2,8,1024]{3,2,1,0:T(8,128)(2,1)S(1)} %bitcast.28, bf16[48,256]{1,0:T(8,128)(2,1)S(1)} %mul.201.wi.vi, bf16[16,256,48]{2,1,0:T(8,128)(2,1)S(1)} %copy-done.1, ...), custom_call_target="tpu_custom_call" | custom-call | tf_op jit(solution)/shard_map/pallas_call | solution.py:203
  40.7 0.6 copy-done.8
  41.3 8.1 %shard_map.173.tot = f32[16,128]{1,0:T(8,128)} custom-call(f32[16,128]{1,0:T(8,128)} %copy-done.8), custom_call_target="tpu_custom_call" | custom-call | tf_op jit(solution)/shard_map/pallas_call | solution.py:264
  49.5 0.6 copy-done.9
  50.1 0.7 copy-done.6
  50.8 33.7 %shard_map.174 = (bf16[64,8,128]{2,1,0:T(8,128)(2,1)S(1)}, f32[16,128]{1,0:T(8,128)S(1)}) custom-call(s32[4]{0:T(128)S(1)} %copy-done.9, f32[2]{0:T(128)S(1)} %copy-done.10, bf16[64,8,128]{2,1,0:T(8,128)(2,1)S(1)} %get-tuple-element.10.sp, f32[16,128]{1,0:T(8,128)S(1)} %copy-done.6, f32[16,128]{1,0:T(8,128)S(1)} %tile.48.spread, ...), custom_call_target="tpu_custom_call" | custom-call | tf_op jit(solution)/shard_map/pallas_call | solution.py:203
  84.4 0.6 copy-done.7
  85.0 8.1 %shard_map.175.tot = f32[16,128]{1,0:T(8,128)} custom-call(f32[16,128]{1,0:T(8,128)} %copy-done.7), custom_call_target="tpu_custom_call" | custom-call | tf_op jit(solution)/shard_map/pallas_call | solution.py:264
  93.2 0.7 copy-done.5
  93.9 17.8 %shard_map.176 = bf16[16,8,512]{2,1,0:T(8,128)(2,1)S(1)} custom-call(s32[4]{0:T(128)S(1)} %copy-done.9, f32[2]{0:T(128)S(1)} %copy-done.10, bf16[64,8,128]{2,1,0:T(8,128)(2,1)S(1)} %get-tuple-element.13.sp, f32[16,128]{1,0:T(8,128)S(1)} %copy-done.5, f32[16,128]{1,0:T(8,128)S(1)} %tile.48.spread, bf16[48,256]{1,0:T(8,128)(2,1)S(1)} %mul.212.wi, ...), custom_call_target="tpu_custom_call" | custom-call | tf_op jit(solution)/shard_map/pallas_call | solution.py:203
  111.6 12.8 %all_to_all.15 = bf16[16,1,8,1,512]{4,2,3,1,0:T(8,128)(2,1)S(1)} all-to-all(bf16[16,1,8,1,512]{4,2,3,1,0:T(8,128)(2,1)S(1)} %bitcast.27), channel_id=1, replica_groups=mesh['group'=2,'shot'=4,'line'=2,'tm'=2] {'shot','line','tm'}, dimensions={0} | all-to-all | bytes 262144 | tf_op jit(solution)/shard_map/all_to_all | solution.py:410
  124.5 0.7 copy.57
  (69 shorter events, 1.5 us)
Async XLA Ops:
  1.2 5.1 %copy-start.19 = (s32[4]{0:T(128)S(1)}, s32[4]{0:T(128)}, u32[]{:S(2)}) copy-start(s32[4]{0:T(128)} %param.21) | copy-start | bytes 52
  1.2 5.3 %copy-start.18 = (s32[8]{0:T(128)S(1)}, s32[8]{0:T(128)}, u32[]{:S(2)}) copy-start(s32[8]{0:T(128)} %param.22) | copy-start | bytes 100
  1.2 5.5 %copy-start.12 = (bf16[4,3,64]{2,0,1:T(4,128)(2,1)S(1)}, bf16[4,3,64]{2,0,1:T(4,128)(2,1)}, u32[]{:S(2)}) copy-start(bf16[4,3,64]{2,0,1:T(4,128)(2,1)} %param.23) | copy-start | bytes 4612
  1.2 5.6 %copy-start.13 = (bf16[4,3,64]{2,0,1:T(4,128)(2,1)S(1)}, bf16[4,3,64]{2,0,1:T(4,128)(2,1)}, u32[]{:S(2)}) copy-start(bf16[4,3,64]{2,0,1:T(4,128)(2,1)} %param.27) | copy-start | bytes 4612
  1.3 6.0 %copy-start.14 = (bf16[4,64]{1,0:T(4,128)(2,1)S(1)}, bf16[4,64]{1,0:T(4,128)(2,1)}, u32[]{:S(2)}) copy-start(bf16[4,64]{1,0:T(4,128)(2,1)} %param.29) | copy-start | bytes 1540
  1.3 6.0 %copy-start.15 = (bf16[4,64]{1,0:T(4,128)(2,1)S(1)}, bf16[4,64]{1,0:T(4,128)(2,1)}, u32[]{:S(2)}) copy-start(bf16[4,64]{1,0:T(4,128)(2,1)} %param.25) | copy-start | bytes 1540
  1.3 6.4 %copy-start.11 = (bf16[1,128,512]{2,1,0:T(8,128)(2,1)S(1)}, bf16[1,128,512]{2,1,0:T(8,128)(2,1)}, u32[]{:S(2)}) copy-start(bf16[1,128,512]{2,1,0:T(8,128)(2,1)} %param.18) | copy-start | bytes 393220
  1.9 21.9 %copy-start.1 = (bf16[16,256,48]{2,1,0:T(8,128)(2,1)S(1)}, bf16[16,256,48]{2,1,0:T(8,128)(2,1)}, u32[]{:S(2)}) copy-start(bf16[16,256,48]{2,1,0:T(8,128)(2,1)} %constant.70.clone.wp.vp) | copy-start | bytes 1179652
  1.9 8.5 %all-to-all-start.1 = ((bf16[2,2,8,1,1024]{4,2,1,3,0:T(8,128)(2,1)}), bf16[2,2,8,1,1024]{4,2,1,3,0:T(8,128)(2,1)S(1)}, u32[]{:S(2)}, u32[]{:S(2)}) async-start(bf16[2,2,8,1,1024]{4,2,1,3,0:T(8,128)(2,1)} %pad_maximum_fusion), calls=%async_computation.1 | async-start | bytes 131072 | tf_op jit(solution)/shard_map/all_to_all | solution.py:311
  10.4 13.5 %all-to-all-start = ((bf16[16,1,8,1,512]{4,2,3,1,0:T(8,128)(2,1)}), bf16[16,1,8,1,512]{4,2,3,1,0:T(8,128)(2,1)S(1)}, u32[]{:S(2)}, u32[]{:S(2)}) async-start(bf16[16,1,8,1,512]{4,2,3,1,0:T(8,128)(2,1)} %copy.46), calls=%async_computation | async-start | bytes 262144 | tf_op jit(solution)/shard_map/all_to_all | solution.py:294
  16.2 0.7 copy-start.16
  16.2 1.6 %copy-start.17 = (f32[2,64]{1,0:T(2,128)S(1)}, f32[2,64]{1,0:T(2,128)}, u32[]{:S(2)}) copy-start(f32[2,64]{1,0:T(2,128)} %param.30) | copy-start | bytes 1540
  16.2 7.6 %copy-start.3 = (bf16[3,64,64]{2,1,0:T(8,128)(2,1)S(1)}, bf16[3,64,64]{2,1,0:T(8,128)(2,1)}, u32[]{:S(2)}) copy-start(bf16[3,64,64]{2,1,0:T(8,128)(2,1)} %vm.1) | copy-start | bytes 73732
  16.9 7.0 %copy-start.2 = (bf16[16,16,256]{2,1,0:T(8,128)(2,1)S(1)}, bf16[16,16,256]{2,1,0:T(8,128)(2,1)}, u32[]{:S(2)}) copy-start(bf16[16,16,256]{2,1,0:T(8,128)(2,1)} %constant.71.clone.wq.vq) | copy-start | bytes 393220
  17.0 32.5 %copy-start = (bf16[16,256,48]{2,1,0:T(8,128)(2,1)S(1)}, bf16[16,256,48]{2,1,0:T(8,128)(2,1)}, u32[]{:S(2)}) copy-start(bf16[16,256,48]{2,1,0:T(8,128)(2,1)} %constant.72.clone.wp) | copy-start | bytes 1179652
  23.8 25.6 %copy-start.4 = (bf16[3,64,64]{2,1,0:T(8,128)(2,1)S(1)}, bf16[3,64,64]{2,1,0:T(8,128)(2,1)}, u32[]{:S(2)}) copy-start(bf16[3,64,64]{2,1,0:T(8,128)(2,1)} %wm.5) | copy-start | bytes 73732
  40.7 0.6 copy-start.8
  49.4 0.7 copy-start.9
  49.4 0.7 copy-start.10
  50.1 0.7 copy-start.6
  84.4 0.6 copy-start.7
  93.2 0.7 copy-start.5

commit v3 on v2

--- a/solution.py
+++ b/solution.py
@@ -144,8 +144,11 @@
     sort, each = by_phase(width), C // halves
 
     def traces(c):
-        at, t = slice(c % each * width, (c % each + 1) * width), c // each
-        rows = [x[(s * blocks + b) * halves + t, :, at].astype(F32) for s in range(shots) for b in range(blocks)]
+        t, fold, lh = c // each, each // 2, x.shape[1] // 2
+        row, at = c % each // fold * lh, slice(c % fold * width, (c % fold + 1) * width)
+        rows = [
+            x[(s * blocks + b) * halves + t].astype(F32)[row : row + lh, at] for s in range(shots) for b in range(blocks)
+        ]
         return jnp.concatenate(rows, axis=0).astype(BF16)
 
     def records(c):
@@ -169,14 +172,16 @@
         shots, sp[...].astype(F32), tot, spread, (wi, wp, wm, wo, wq, bi), lags, join, mix, take, pace[it], buf, total, band
     )
     cube[...] = x.astype(F32)
-    n, lh = cube.shape[2] // 2, out.shape[1]
+    n, lh = cube.shape[2] // 2, out.shape[1] // 2
+    fold = each // 2
     for c in range(C):
         v = cube[:, c, :]
         v = jnp.concatenate([v[:, :n], v[:, n:]], axis=0).T.astype(BF16)
         v = jnp.dot(v, sort, preferred_element_type=F32)
-        at, t = slice(c % each * width, (c % each + 1) * width), c // each
+        t = c // each
+        row, at = c % each // fold * lh, slice(c % fold * width, (c % fold + 1) * width)
         for j in range(shots * blocks):
-            out[j * halves + t, :, at] = v[j * lh : (j + 1) * lh].astype(BF16)
+            out[j * halves + t, row : row + lh, at] = v[j * lh : (j + 1) * lh].astype(BF16)
 
 
 def first_kernel(x, wi, wp, wm, wo, wq, bi, member, out, part, total, band):
@@ -224,30 +229,72 @@
     return rows, jnp.asarray(pick, BF16), w_mid, ends, jnp.asarray(place, BF16), jnp.tile(bias, (1, PACK))
 
 
-def exchange_kernel(sizes, x, out, slots, send, recv):
+def greeted(sizes):
     count = math.prod(sizes)
     me = (lax.axis_index("shot") * sizes[1] + lax.axis_index("line")) * sizes[2] + lax.axis_index("tm")
-
-    def peer(off):
+    peers = []
+    for off in range(1, count):
         at = lax.rem(me + off, count)
-        return {
+        coords = {
             "shot": at // (sizes[1] * sizes[2]),
             "line": lax.rem(at // sizes[2], sizes[1]),
             "tm": lax.rem(at, sizes[2]),
         }
-
+        peers.append((off, at, coords))
     barrier = pltpu.get_barrier_semaphore()
-    for off in range(1, count):
-        pl.semaphore_signal(barrier, inc=1, device_id=peer(off), device_id_type=pl.DeviceIdType.MESH)
+    for _, _, coords in peers:
+        pl.semaphore_signal(barrier, inc=1, device_id=coords, device_id_type=pl.DeviceIdType.MESH)
     pl.semaphore_wait(barrier, count - 1)
+    return me, peers
+
+
+def swap_kernel(sizes, x, out, slots, send, recv):
+    me, peers = greeted(sizes)
+    count = math.prod(sizes)
     copies = []
-    for off in range(1, count):
+    for off, at, coords in peers:
+        copy = pltpu.make_async_remote_copy(
+            src_ref=x.at[at],
+            dst_ref=slots.at[off],
+            send_sem=send.at[off],
+            recv_sem=recv.at[off],
+            device_id=coords,
+            device_id_type=pl.DeviceIdType.MESH,
+        )
+        copy.start()
+        copies.append(copy)
+    out[me] = x[me]
+    for off, copy in enumerate(copies, 1):
+        copy.wait()
+        out[lax.rem(me + count - off, count)] = slots[off]
+
+
+def swapped(x, sizes):
+    count, v = math.prod(sizes), pl.BlockSpec(memory_space=pltpu.VMEM)
+    return pl.pallas_call(
+        functools.partial(swap_kernel, sizes),
+        out_shape=jax.ShapeDtypeStruct(x.shape, x.dtype),
+        in_specs=[v],
+        out_specs=v,
+        scratch_shapes=[
+            pltpu.VMEM(x.shape, x.dtype),
+            pltpu.SemaphoreType.DMA((count,)),
+            pltpu.SemaphoreType.DMA((count,)),
+        ],
+        compiler_params=pltpu.CompilerParams(collective_id=1, has_side_effects=True),
+    )(x)
+
+
+def exchange_kernel(sizes, x, out, slots, send, recv):
+    _, peers = greeted(sizes)
+    copies = []
+    for off, _, coords in peers:
         copy = pltpu.make_async_remote_copy(
             src_ref=x,
             dst_ref=slots.at[off],
             send_sem=send.at[off],
             recv_sem=recv.at[off],
-            device_id=peer(off),
+            device_id=coords,
             device_id_type=pl.DeviceIdType.MESH,
         )
         copy.start()
@@ -290,12 +337,14 @@
     sources = n_shot if whole else 1
     i32 = functools.partial(jnp.arange, dtype=jnp.int32)
 
-    x = guess.reshape(sh, lh, parts, kp, tl).transpose(2, 0, 1, 3, 4)
-    x = lax.all_to_all(x, where, split_axis=0, concat_axis=0)
-    fused = whole and sh == 1 and kp == 1 and C % n_tm == 0
+    fused = whole and sh == 1 and kp == 1 and C % (2 * n_tm) == 0 and 2 * lh % 16 == 0
+    sizes = (n_shot, n_line, n_tm)
     if fused:
-        x = x.reshape(parts, lh, tl)
+        x = guess.reshape(lh, parts, 2, tl // 2).transpose(1, 2, 0, 3).reshape(parts, 2 * lh, tl // 2)
+        x = swapped(x, sizes)
     else:
+        x = guess.reshape(sh, lh, parts, kp, tl).transpose(2, 0, 1, 3, 4)
+        x = lax.all_to_all(x, where, split_axis=0, concat_axis=0)
         x = x.reshape(sources, n_line, n_tm, sh, lh, kp, tl).transpose(0, 3, 1, 4, 5, 2, 6)
         x = x.reshape(s1, r1, C, planes, 2).transpose(3, 2, 4, 0, 1).reshape(planes, C, lanes1)
 
@@ -395,7 +444,7 @@
             )
             continue
         if fused:
-            back = jax.ShapeDtypeStruct((parts, lh, tl), BF16)
+            back = jax.ShapeDtypeStruct((parts, 2 * lh, tl // 2), BF16)
             x = call(functools.partial(exit_kernel, it, dims), back, ins, 2, [buf, tot2, band, cube])
             continue
         x = call(functools.partial(station_kernel, it, shots), moved, ins, 2, [buf, tot2, band])
@@ -404,6 +453,9 @@
             if it < ITERS - 1:
                 sp, energy = call(first_kernel, (spass, part), (x, *wa, member), 0, [tot1, band])
 
+    if fused:
+        x = swapped(x, sizes).reshape(parts, 2, lh, tl // 2)
+        return x.transpose(2, 0, 1, 3).reshape(sh, recv, tl)
     if not fused:
         x = x.reshape(planes, C, 2, s1, r1).transpose(3, 4, 1, 0, 2)
         x = x.reshape(sources, sh, n_line, lh, kp, n_tm, tl).transpose(0, 2, 5, 1, 3, 4, 6)

time: 126 us -> 126 us (level)
  Pallas kernels: 84.5 us -> 107 us
  blocking collectives: 12.8 us -> 0 us
  waiting for transfers between devices: 7.9 us -> 0.01 us
  starting transfers between devices: 9.85 us -> 4.21 us
  local copies, waits for them, and re-layouts: 8.06 us -> 12.6 us
    pallas_call x0 -> x2, Pallas kernels: none -> 20 us  [swapped(): pl.pallas_call(functools.partial(swap_kernel, sizes), out_shape=jax.Shape...]
    all_to_all x1 -> x0, blocking collectives: 12.8 us -> none  [per_device(): lax.all_to_all(x.reshape(parts, sh, lh, kp, tl), where, split_axis=0, con...]
    all_to_all x1 -> x0, waiting for transfers between devices: 5.96 us -> none  [per_device(): x = lax.all_to_all(x, where, split_axis=0, concat_axis=0)]
    all_to_all x1 -> x0, starting transfers between devices: 5.51 us -> none  [per_device(): x = lax.all_to_all(x, where, split_axis=0, concat_axis=0)]
    unnamed x42 -> x46, local copies, waits for them, and re-layouts: 3.85 us -> 7.33 us
    pallas_call x2, Pallas kernels: 16.2 us -> 18.6 us  [summed(): pl.pallas_call(functools.partial(exchange_kernel, sizes), out_shape=jax.S...]
    all_to_all x1, waiting for transfers between devices: 1.95 us -> 0.01 us  [per_device(): m = lax.all_to_all(sent, 'line', split_axis=0, concat_axis=0)]
    reshape x0 -> x3, local copies, waits for them, and re-layouts: none -> 1.51 us  [the longest x2 0.77 us: per_device(): guess.reshape(lh, parts, 2, tl // 2).transpose(1, 2, 0, 3)]
  transfers between devices with their start and end apart: 2 -> 1, of which waited for: 2 -> 0; matrix products, arithmetic and copies ran while one was open for 3% -> 3% of each run, Pallas kernels for 0% -> 8%
where the time goes in v3:
time: 126 us
  Pallas kernels  107 us (85%)
  local copies, waits for them, and re-layouts  12.6 us (10%)
  starting transfers between devices  4.21 us (3%)
  other arithmetic  1.74 us (1%)
    pallas_call x3, Pallas kernels, call(): pl.pallas_call(body, out_shape=outs, in_specs=[s] * smem + [v] * (len(ins...  68.3 us
    pallas_call x2, Pallas kernels, swapped(): pl.pallas_call(functools.partial(swap_kernel, sizes), out_shape=jax.Shape...  20 us
    pallas_call x2, Pallas kernels, summed(): pl.pallas_call(functools.partial(exchange_kernel, sizes), out_shape=jax.S...  18.6 us
    unnamed x46, local copies, waits for them, and re-layouts  7.33 us
    all_to_all x1, starting transfers between devices, per_device(): m = lax.all_to_all(sent, 'line', split_axis=0, concat_axis=0)  4.21 us
  transfers between devices with their start and end apart: 1, of which 0 were waited for; matrix products, arithmetic and copies ran while one was open for 3% of the time, Pallas kernels for 8%

profile of v3, /device:TPU:0, one launch (start us, length us, event | category | flops | bytes accessed | tf_op | source)
XLA Modules:
  0.0 125.8 jit_solution(12275432706435670608)
XLA Ops:
  0.0 1.2 constant_dynamic-slice_fusion.1
  1.2 0.6 pad_maximum_fusion
  1.8 4.2 %all-to-all-start = ((bf16[2,2,8,1,1024]{4,2,1,3,0:T(8,128)(2,1)}), bf16[2,2,8,1,1024]{4,2,1,3,0:T(8,128)(2,1)S(1)}, u32[]{:S(2)}, u32[]{:S(2)}) async-start(bf16[2,2,8,1,1024]{4,2,1,3,0:T(8,128)(2,1)} %pad_maximum_fusion), calls=%async_computation | async-start | bytes 131072 | tf_op jit(solution)/shard_map/all_to_all | solution.py:360
  6.1 0.6 copy-done.21
  6.7 0.1 select_reduce_fusion.1
  6.9 0.6 copy-done.20
  7.6 0.1 select_reduce_fusion
  7.7 0.1 copy.51
  7.8 0.5 copy-done.14
  8.4 0.7 copy-done.15
  9.6 0.1 broadcast_multiply_fusion
  10.0 0.1 broadcast_multiply_fusion.2
  10.3 0.1 mul.201.wi.vi
  10.5 0.1 copy.52.wo.vo
  10.8 0.7 copy.63
  11.5 10.4 %shard_map.172.x = bf16[16,16,256]{2,1,0:T(8,128)(2,1)} custom-call(bf16[16,16,256]{2,1,0:T(8,128)(2,1)} %bitcast.25), custom_call_target="tpu_custom_call" | custom-call | tf_op jit(solution)/shard_map/pallas_call | solution.py:274
  22.4 0.1 copy.54.wo
  22.7 0.9 copy-done.3
  23.6 16.8 %shard_map.173 = (bf16[64,8,128]{2,1,0:T(8,128)(2,1)S(1)}, f32[16,128]{1,0:T(8,128)S(1)}, bf16[512,64]{1,0:T(8,128)(2,1)S(1)}) custom-call(bf16[16,16,256]{2,1,0:T(8,128)(2,1)S(1)} %copy-done.3, bf16[2,2,8,1024]{3,2,1,0:T(8,128)(2,1)S(1)} %bitcast.24, bf16[48,256]{1,0:T(8,128)(2,1)S(1)} %mul.201.wi.vi, bf16[16,256,48]{2,1,0:T(8,128)(2,1)S(1)} %copy-done.1, ...), custom_call_target="tpu_custom_call" | custom-call | tf_op jit(solution)/shard_map/pallas_call | solution.py:208
  40.4 0.6 copy-done.10
  41.0 9.3 %shard_map.174.tot = f32[16,128]{1,0:T(8,128)} custom-call(f32[16,128]{1,0:T(8,128)} %copy-done.10), custom_call_target="tpu_custom_call" | custom-call | tf_op jit(solution)/shard_map/pallas_call | solution.py:311
  50.4 0.6 copy-done.11
  51.0 0.7 copy-done.8
  51.7 33.7 %shard_map.175 = (bf16[64,8,128]{2,1,0:T(8,128)(2,1)S(1)}, f32[16,128]{1,0:T(8,128)S(1)}) custom-call(s32[4]{0:T(128)S(1)} %copy-done.11, f32[2]{0:T(128)S(1)} %copy-done.12, bf16[64,8,128]{2,1,0:T(8,128)(2,1)S(1)} %get-tuple-element.10.sp, f32[16,128]{1,0:T(8,128)S(1)} %copy-done.8, f32[16,128]{1,0:T(8,128)S(1)} %tile.48.spread, ...), custom_call_target="tpu_custom_call" | custom-call | tf_op jit(solution)/shard_map/pallas_call | solution.py:208
  85.4 0.6 copy-done.9
  86.0 9.3 %shard_map.176.tot = f32[16,128]{1,0:T(8,128)} custom-call(f32[16,128]{1,0:T(8,128)} %copy-done.9), custom_call_target="tpu_custom_call" | custom-call | tf_op jit(solution)/shard_map/pallas_call | solution.py:311
  95.3 0.7 copy-done.7
  96.0 17.8 %shard_map.177.x = bf16[16,16,256]{2,1,0:T(8,128)(2,1)S(1)} custom-call(s32[4]{0:T(128)S(1)} %copy-done.11, f32[2]{0:T(128)S(1)} %copy-done.12, bf16[64,8,128]{2,1,0:T(8,128)(2,1)S(1)} %get-tuple-element.13.sp, f32[16,128]{1,0:T(8,128)S(1)} %copy-done.7, f32[16,128]{1,0:T(8,128)S(1)} %tile.48.spread, bf16[48,256]{1,0:T(8,128)(2,1)S(1)} %mul.212.wi, ...), custom_call_target="tpu_custom_call" | custom-call | tf_op jit(solution)/shard_map/pallas_call | solution.py:208
  113.8 0.6 copy-done.4
  114.4 9.6 %shard_map.178 = bf16[16,16,256]{2,1,0:T(8,128)(2,1)} custom-call(bf16[16,16,256]{2,1,0:T(8,128)(2,1)} %copy-done.4), custom_call_target="tpu_custom_call" | custom-call | tf_op jit(solution)/shard_map/pallas_call | solution.py:274
  124.0 1.0 copy.57
  125.0 0.7 reshape.345
  (74 shorter events, 1.9 us)
Async XLA Ops:
  1.8 20.8 %all-to-all-start = ((bf16[2,2,8,1,1024]{4,2,1,3,0:T(8,128)(2,1)}), bf16[2,2,8,1,1024]{4,2,1,3,0:T(8,128)(2,1)S(1)}, u32[]{:S(2)}, u32[]{:S(2)}) async-start(bf16[2,2,8,1,1024]{4,2,1,3,0:T(8,128)(2,1)} %pad_maximum_fusion), calls=%async_computation | async-start | bytes 131072 | tf_op jit(solution)/shard_map/all_to_all | solution.py:360
  6.1 0.7 copy-start.21
  6.9 0.7 copy-start.20
  7.7 0.7 copy-start.14
  8.4 0.7 copy-start.15
  9.2 0.7 copy-start.16
  9.2 0.7 copy-start.17
  9.2 1.4 %copy-start.18 = (f32[2,64]{1,0:T(2,128)S(1)}, f32[2,64]{1,0:T(2,128)}, u32[]{:S(2)}) copy-start(f32[2,64]{1,0:T(2,128)} %param.26) | copy-start | bytes 1540
  9.2 1.5 %copy-start.13 = (bf16[1,128,512]{2,1,0:T(8,128)(2,1)S(1)}, bf16[1,128,512]{2,1,0:T(8,128)(2,1)}, u32[]{:S(2)}) copy-start(bf16[1,128,512]{2,1,0:T(8,128)(2,1)} %param.18) | copy-start | bytes 393220
  9.3 13.3 %copy-start.1 = (bf16[16,256,48]{2,1,0:T(8,128)(2,1)S(1)}, bf16[16,256,48]{2,1,0:T(8,128)(2,1)}, u32[]{:S(2)}) copy-start(bf16[16,256,48]{2,1,0:T(8,128)(2,1)} %constant.70.clone.wp.vp) | copy-start | bytes 1179652
  11.5 11.1 %copy-start.19 = (f32[2,64]{1,0:T(2,128)S(1)}, f32[2,64]{1,0:T(2,128)}, u32[]{:S(2)}) copy-start(f32[2,64]{1,0:T(2,128)} %param.30) | copy-start | bytes 1540
  11.5 11.2 %copy-start.2 = (bf16[16,16,256]{2,1,0:T(8,128)(2,1)S(1)}, bf16[16,16,256]{2,1,0:T(8,128)(2,1)}, u32[]{:S(2)}) copy-start(bf16[16,16,256]{2,1,0:T(8,128)(2,1)} %constant.71.clone.wq.vq) | copy-start | bytes 393220
  11.5 11.2 %copy-start.5 = (bf16[3,64,64]{2,1,0:T(8,128)(2,1)S(1)}, bf16[3,64,64]{2,1,0:T(8,128)(2,1)}, u32[]{:S(2)}) copy-start(bf16[3,64,64]{2,1,0:T(8,128)(2,1)} %vm.1) | copy-start | bytes 73732
  21.9 28.4 %copy-start = (bf16[16,256,48]{2,1,0:T(8,128)(2,1)S(1)}, bf16[16,256,48]{2,1,0:T(8,128)(2,1)}, u32[]{:S(2)}) copy-start(bf16[16,256,48]{2,1,0:T(8,128)(2,1)} %constant.72.clone.wp) | copy-start | bytes 1179652
  22.7 0.9 copy-start.3
  23.6 26.8 %copy-start.6 = (bf16[3,64,64]{2,1,0:T(8,128)(2,1)S(1)}, bf16[3,64,64]{2,1,0:T(8,128)(2,1)}, u32[]{:S(2)}) copy-start(bf16[3,64,64]{2,1,0:T(8,128)(2,1)} %wm.5) | copy-start | bytes 73732
  40.4 0.6 copy-start.10
  50.3 0.7 copy-start.11
  50.3 0.7 copy-start.12
  51.0 0.7 copy-start.8
  85.4 0.6 copy-start.9
  95.3 0.7 copy-start.7
  113.8 0.7 copy-start.4

commit v4 on v2

--- a/solution.py
+++ b/solution.py
@@ -137,7 +137,7 @@
 
 
 def entry_kernel(
-    dims, x, m, wi, wp, wm, wo, wq, bi, member, out, part, mix, total, band, cube, side
+    dims, x, wi, wp, wm, wo, wq, bi, member, out, part, mix, total, band, cube, side
 ):
     shots, blocks, halves = dims
     width = 2 * cube.shape[0]
@@ -148,9 +148,15 @@
         rows = [x[(s * blocks + b) * halves + t, :, at].astype(F32) for s in range(shots) for b in range(blocks)]
         return jnp.concatenate(rows, axis=0).astype(BF16)
 
+    tl = each * width
+
     def records(c):
-        at = slice(c * width, (c + 1) * width)
-        rows = [m[b, g, :, at].astype(F32) for g in range(m.shape[1]) for b in range(blocks)]
+        s, t = c // halves, c % halves
+        rows = [
+            x[(s * blocks + b) * halves + t, :, tl + g * width : tl + (g + 1) * width].astype(F32)
+            for g in range((x.shape[2] - tl) // width)
+            for b in range(blocks)
+        ]
         return jnp.concatenate(rows, axis=0).astype(BF16)
 
     unfold(records, side, sort)
@@ -290,28 +296,29 @@
     sources = n_shot if whole else 1
     i32 = functools.partial(jnp.arange, dtype=jnp.int32)
 
+    at_shot = lax.axis_index("shot")
+    n_mix, run = mixtures.shape[0], nt // C
+    fused = whole and sh == 1 and kp == 1 and C % n_tm == 0 and n_shot * n_tm == C
     x = guess.reshape(sh, lh, parts, kp, tl).transpose(2, 0, 1, 3, 4)
-    x = lax.all_to_all(x, where, split_axis=0, concat_axis=0)
-    fused = whole and sh == 1 and kp == 1 and C % n_tm == 0
     if fused:
-        x = x.reshape(parts, lh, tl)
-    else:
+        share = (at_shot * n_tm + lax.axis_index("tm")) * run
+        mine = lax.dynamic_slice_in_dim(mixtures, share, run, axis=2).reshape(n_mix, lh, parts, run)
+        mine = mine.transpose(2, 1, 0, 3).reshape(parts, lh, n_mix * run)
+        x = jnp.concatenate([x.reshape(parts, lh, tl), mine], axis=2)
+    x = lax.all_to_all(x, where, split_axis=0, concat_axis=0, tiled=False)
+    if not fused:
         x = x.reshape(sources, n_line, n_tm, sh, lh, kp, tl).transpose(0, 3, 1, 4, 5, 2, 6)
         x = x.reshape(s1, r1, C, planes, 2).transpose(3, 2, 4, 0, 1).reshape(planes, C, lanes1)
 
-    at_shot = lax.axis_index("shot")
 
     def first_k(line):
         block = line * n_tm + lax.axis_index("tm")
         return (at_shot * n_line * n_tm + block if whole else block) * kp
 
-    n_mix = mixtures.shape[0]
-    grid = mixtures.reshape(n_mix, lh, RPL, nt)
-    sent = jnp.stack([lax.dynamic_slice_in_dim(grid, first_k(d), kp, axis=2) for d in range(n_line)])
-    m = lax.all_to_all(sent, "line", split_axis=0, concat_axis=0)
-    if fused:
-        m = m.reshape(n_line, n_mix, lh, nt)
-    else:
+    if not fused:
+        grid = mixtures.reshape(n_mix, lh, RPL, nt)
+        sent = jnp.stack([lax.dynamic_slice_in_dim(grid, first_k(d), kp, axis=2) for d in range(n_line)])
+        m = lax.all_to_all(sent, "line", split_axis=0, concat_axis=0)
         m = m.transpose(1, 0, 2, 3, 4).reshape(n_mix, r1, nt)
         if not whole:
             m = lax.dynamic_slice_in_dim(m, at_shot * r2, r2, axis=1)
@@ -378,7 +385,7 @@
         sp, energy, m = call(
             functools.partial(entry_kernel, dims),
             (spass, part, mixed),
-            (x, m, *wa, member),
+            (x, *wa, member),
             0,
             [tot1, band, cube, side],
         )

time: 126 us -> 122 us (0.968)
  waiting for transfers between devices: 7.9 us -> 3.67 us
  local copies, waits for them, and re-layouts: 8.06 us -> 10.6 us
  starting transfers between devices: 9.85 us -> 7.36 us
    all_to_all x2 -> x1, waiting for transfers between devices: 7.9 us -> 3.67 us  [per_device(): x = lax.all_to_all(x, where, split_axis=0, concat_axis=0, tiled=False)]
    unnamed x42 -> x50, local copies, waits for them, and re-layouts: 3.85 us -> 7.08 us
    all_to_all x2 -> x1, starting transfers between devices: 9.85 us -> 7.36 us  [per_device(): x = lax.all_to_all(x, where, split_axis=0, concat_axis=0, tiled=False)]
  transfers between devices with their start and end apart: 2 -> 1, of which waited for: 2 -> 1; matrix products, arithmetic and copies ran while one was open for 3% -> 3% of each run, Pallas kernels for 0% -> 0%
where the time goes in v4:
time: 122 us; the launch traced here: 121 us
  Pallas kernels  84.4 us (69%)
  blocking collectives  12.8 us (10%)
  local copies, waits for them, and re-layouts  10.6 us (9%)
  starting transfers between devices  7.36 us (6%)
  waiting for transfers between devices  3.67 us (3%)
  other arithmetic  1.81 us (1%)
    pallas_call x3, Pallas kernels, call(): pl.pallas_call(body, out_shape=outs, in_specs=[s] * smem + [v] * (len(ins...  68.2 us
    pallas_call x2, Pallas kernels, summed(): pl.pallas_call(functools.partial(exchange_kernel, sizes), out_shape=jax.S...  16.2 us
    all_to_all x1, blocking collectives, per_device(): lax.all_to_all(x.reshape(parts, sh, lh, kp, tl), where, split_axis=0, con...  12.8 us
    all_to_all x1, starting transfers between devices, per_device(): x = lax.all_to_all(x, where, split_axis=0, concat_axis=0, tiled=False)  7.36 us
    unnamed x50, local copies, waits for them, and re-layouts  7.08 us
    all_to_all x1, waiting for transfers between devices, per_device(): x = lax.all_to_all(x, where, split_axis=0, concat_axis=0, tiled=False)  3.67 us
  transfers between devices with their start and end apart: 1, of which 1 were waited for; matrix products, arithmetic and copies ran while one was open for 3% of the time, Pallas kernels for 0%

profile of v4, /device:TPU:0, one launch (start us, length us, event | category | flops | bytes accessed | tf_op | source)
XLA Modules:
  0.0 121.1 jit_solution(15744677346640708935)
XLA Ops:
  0.0 1.0 copy-done
  1.1 0.9 copy-done.15
  2.1 0.7 pad_maximum_fusion
  2.7 7.4 %all-to-all-start = ((bf16[16,8,768]{2,1,0:T(8,128)(2,1)}), bf16[16,8,768]{2,1,0:T(8,128)(2,1)S(1)}, u32[]{:S(2)}, u32[]{:S(2)}) async-start(bf16[16,8,768]{2,1,0:T(8,128)(2,1)} %pad_maximum_fusion), calls=%async_computation | async-start | bytes 393216 | tf_op jit(solution)/shard_map/all_to_all | solution.py:308
  10.2 0.1 select_reduce_fusion.1
  10.4 0.1 select_reduce_fusion
  10.7 0.1 copy.45
  10.9 0.1 broadcast_multiply_fusion.2
  11.0 0.1 mul.204.wi.vi
  11.1 0.6 copy-done.19
  11.7 0.1 copy-done.18
  12.0 0.1 copy.46.wo.vo
  12.1 0.6 copy-done.20
  12.7 0.7 tile.19.bi.ci
  13.8 0.1 broadcast_multiply_fusion
  14.4 0.1 mul.216.wi
  14.6 0.1 copy.48.wo
  14.8 0.7 tile.50.bi
  15.4 3.7 %all-to-all-done.x = bf16[16,8,768]{2,1,0:T(8,128)(2,1)S(1)} async-done(((bf16[16,8,768]{2,1,0:T(8,128)(2,1)}), bf16[16,8,768]{2,1,0:T(8,128)(2,1)S(1)}, u32[]{:S(2)}, u32[]{:S(2)}) %all-to-all-start) | async-done | bytes 196640 | tf_op jit(solution)/shard_map/all_to_all | solution.py:308
  19.1 0.7 copy-done.8
  19.8 16.8 %shard_map.172 = (bf16[64,8,128]{2,1,0:T(8,128)(2,1)S(1)}, f32[16,128]{1,0:T(8,128)S(1)}, bf16[512,64]{1,0:T(8,128)(2,1)S(1)}) custom-call(bf16[16,8,768]{2,1,0:T(8,128)(2,1)S(1)} %all-to-all-done.x, bf16[48,256]{1,0:T(8,128)(2,1)S(1)} %mul.204.wi.vi, bf16[16,256,48]{2,1,0:T(8,128)(2,1)S(1)} %copy-done.2, bf16[3,64,64]{2,1,0:T(8,128)(2,1)S(1)} %copy-done.4, ...), custom_call_target="tpu_custom_call" | custom-call | tf_op jit(solution)/shard_map/pallas_call | solution.py:209
  36.6 0.6 copy-done.12
  37.2 8.1 %shard_map.173.tot = f32[16,128]{1,0:T(8,128)} custom-call(f32[16,128]{1,0:T(8,128)} %copy-done.12), custom_call_target="tpu_custom_call" | custom-call | tf_op jit(solution)/shard_map/pallas_call | solution.py:270
  45.4 0.6 copy-done.9
  46.0 0.7 copy-done.7
  46.7 33.6 %shard_map.174 = (bf16[64,8,128]{2,1,0:T(8,128)(2,1)S(1)}, f32[16,128]{1,0:T(8,128)S(1)}) custom-call(s32[4]{0:T(128)S(1)} %copy-done.13, f32[2]{0:T(128)S(1)} %copy-done.14, bf16[64,8,128]{2,1,0:T(8,128)(2,1)S(1)} %get-tuple-element.10.sp, f32[16,128]{1,0:T(8,128)S(1)} %copy-done.7, f32[16,128]{1,0:T(8,128)S(1)} %tile.48.spread, ...), custom_call_target="tpu_custom_call" | custom-call | tf_op jit(solution)/shard_map/pallas_call | solution.py:209
  80.4 0.6 copy-done.11
  81.0 8.1 %shard_map.175.tot = f32[16,128]{1,0:T(8,128)} custom-call(f32[16,128]{1,0:T(8,128)} %copy-done.11), custom_call_target="tpu_custom_call" | custom-call | tf_op jit(solution)/shard_map/pallas_call | solution.py:270
  89.1 0.7 copy-done.6
  89.8 17.8 %shard_map.176 = bf16[16,8,512]{2,1,0:T(8,128)(2,1)S(1)} custom-call(s32[4]{0:T(128)S(1)} %copy-done.13, f32[2]{0:T(128)S(1)} %copy-done.14, bf16[64,8,128]{2,1,0:T(8,128)(2,1)S(1)} %get-tuple-element.13.sp, f32[16,128]{1,0:T(8,128)S(1)} %copy-done.6, f32[16,128]{1,0:T(8,128)S(1)} %tile.48.spread, bf16[48,256]{1,0:T(8,128)(2,1)S(1)} %mul.216.wi, ...), custom_call_target="tpu_custom_call" | custom-call | tf_op jit(solution)/shard_map/pallas_call | solution.py:209
  107.5 12.8 %all_to_all.10 = bf16[16,1,8,1,512]{4,2,3,1,0:T(8,128)(2,1)S(1)} all-to-all(bf16[16,1,8,1,512]{4,2,3,1,0:T(8,128)(2,1)S(1)} %bitcast.28), channel_id=1, replica_groups=mesh['group'=2,'shot'=4,'line'=2,'tm'=2] {'shot','line','tm'}, dimensions={0} | all-to-all | bytes 262144 | tf_op jit(solution)/shard_map/all_to_all | solution.py:417
  120.4 0.7 copy.52
  (75 shorter events, 1.7 us)
Async XLA Ops:
  0.0 1.0 copy-start
  1.0 0.9 copy-start.15
  1.9 8.2 %copy-start.23 = (s32[4]{0:T(128)S(1)}, s32[4]{0:T(128)}, u32[]{:S(2)}) copy-start(s32[4]{0:T(128)} %param.21) | copy-start | bytes 52
  1.9 8.4 %copy-start.22 = (s32[8]{0:T(128)S(1)}, s32[8]{0:T(128)}, u32[]{:S(2)}) copy-start(s32[8]{0:T(128)} %param.22) | copy-start | bytes 100
  2.0 8.9 %copy-start.16 = (bf16[4,3,64]{2,0,1:T(4,128)(2,1)S(1)}, bf16[4,3,64]{2,0,1:T(4,128)(2,1)}, u32[]{:S(2)}) copy-start(bf16[4,3,64]{2,0,1:T(4,128)(2,1)} %param.23) | copy-start | bytes 4612
  2.0 8.9 %copy-start.17 = (bf16[4,3,64]{2,0,1:T(4,128)(2,1)S(1)}, bf16[4,3,64]{2,0,1:T(4,128)(2,1)}, u32[]{:S(2)}) copy-start(bf16[4,3,64]{2,0,1:T(4,128)(2,1)} %param.27) | copy-start | bytes 4612
  2.0 17.1 %copy-start.2 = (bf16[16,256,48]{2,1,0:T(8,128)(2,1)S(1)}, bf16[16,256,48]{2,1,0:T(8,128)(2,1)}, u32[]{:S(2)}) copy-start(bf16[16,256,48]{2,1,0:T(8,128)(2,1)} %constant.73.clone.wp.vp) | copy-start | bytes 1179652
  2.7 16.4 %all-to-all-start = ((bf16[16,8,768]{2,1,0:T(8,128)(2,1)}), bf16[16,8,768]{2,1,0:T(8,128)(2,1)S(1)}, u32[]{:S(2)}, u32[]{:S(2)}) async-start(bf16[16,8,768]{2,1,0:T(8,128)(2,1)} %pad_maximum_fusion), calls=%async_computation | async-start | bytes 393216 | tf_op jit(solution)/shard_map/all_to_all | solution.py:308
  11.0 0.7 copy-start.19
  11.1 0.7 copy-start.18
  12.0 0.7 copy-start.20
  13.6 1.2 copy-start.21
  13.7 5.4 %copy-start.3 = (bf16[16,16,256]{2,1,0:T(8,128)(2,1)S(1)}, bf16[16,16,256]{2,1,0:T(8,128)(2,1)}, u32[]{:S(2)}) copy-start(bf16[16,16,256]{2,1,0:T(8,128)(2,1)} %constant.74.clone.wq.vq) | copy-start | bytes 393220
  13.7 5.4 %copy-start.4 = (bf16[3,64,64]{2,1,0:T(8,128)(2,1)S(1)}, bf16[3,64,64]{2,1,0:T(8,128)(2,1)}, u32[]{:S(2)}) copy-start(bf16[3,64,64]{2,1,0:T(8,128)(2,1)} %vm.1) | copy-start | bytes 73732
  13.8 31.6 %copy-start.1 = (bf16[16,256,48]{2,1,0:T(8,128)(2,1)S(1)}, bf16[16,256,48]{2,1,0:T(8,128)(2,1)}, u32[]{:S(2)}) copy-start(bf16[16,256,48]{2,1,0:T(8,128)(2,1)} %constant.75.clone.wp) | copy-start | bytes 1179652
  19.1 0.7 copy-start.8
  19.8 25.6 %copy-start.5 = (bf16[3,64,64]{2,1,0:T(8,128)(2,1)S(1)}, bf16[3,64,64]{2,1,0:T(8,128)(2,1)}, u32[]{:S(2)}) copy-start(bf16[3,64,64]{2,1,0:T(8,128)(2,1)} %wm.5) | copy-start | bytes 73732
  36.6 0.6 copy-start.12
  37.2 8.2 %copy-start.10 = (f32[2,256]{1,0:T(2,128)S(1)}, f32[2,256]{1,0:T(2,128)}, u32[]{:S(2)}) copy-start(f32[2,256]{1,0:T(2,128)} %tile.50.bi) | copy-start | bytes 6148
  45.3 0.7 copy-start.9
  45.4 0.7 copy-start.13
  45.4 0.7 copy-start.14
  46.0 0.7 copy-start.7
  80.4 0.6 copy-start.11
  89.1 0.7 copy-start.6
